TPU v7x, 256 devices: a whole 4x4x8 slice. The times are simulated.
256 devices in a mesh: row: 8 (over y, core), col: 32 (over x, z).
Axes of the slice: x: 4, y: 4, z: 8, core: 2. Of those that a mesh axis runs over, the one named last changes fastest.
Arguments:
- features: bfloat16 [32768, 128], P(('col', 'row')), may hold values from -6 to 6
- tile_values: bfloat16 [32768, 128, 128], P(('row', 'col')), may hold values from -0.0625 to 0.0625
- tile_rows: int32 [32768], P(('row', 'col')), may hold values from 0 to 31, as said below
- tile_cols: int32 [32768], P(('row', 'col')), may hold values from 0 to 7, as said below
- tile_count: int32 [256], P(('row', 'col')), may hold values from 16 to 128, as said below
- weight_in: bfloat16 [128, 1024], replicated, may hold values from -0.5 to 0.5
- weight_hidden: bfloat16 [1024, 1024], replicated, may hold values from -0.1875 to 0.1875
Outputs:
- hidden_out: bfloat16 [32768, 1024], P(('col', 'row'))
Inputs may be any that keep to these rules, and one draw needn't show every extreme that they name: Within one device's 128 slots (live and ignored alike) the pairs (tile_rows, tile_cols) are all different; tile_rows indexes the 32 block rows of the device's row panel. tile_cols indexes the 8 block columns of the device's column panel. A device's live tiles are its first tile_count slots.
All inputs are finite; a program needn't handle non-finite values.
Results may differ from a plain program's by a relative error of at most 0.008.
Values may be sent and summed in bfloat16 or wider, within the bound.
No kernel may reach another device: no remote copies, remote signals or barrier semaphores. Data moves between devices by JAX's collectives and lax.ppermute only.
A program may use at most 128 MiB of HBM per device.

v0:
```python
import jax
import jax.numpy as jnp
from jax import lax
from jax.sharding import PartitionSpec as P


def tile_products(tiles, source_ids, target_ids, tile_total, source, target_blocks, equation):
    capacity = tiles.shape[0]
    block_rows = tiles.shape[1]
    feature_width = source.shape[1]
    source_blocks = source.reshape(-1, block_rows, feature_width)
    source_count = source_blocks.shape[0]
    group_size = 16

    def group_step(group_index, total):
        first_slot = group_index * group_size
        tile_group = lax.dynamic_slice_in_dim(tiles, first_slot, group_size, 0)
        taken_ids = lax.dynamic_slice_in_dim(source_ids, first_slot, group_size, 0)
        placed_ids = lax.dynamic_slice_in_dim(target_ids, first_slot, group_size, 0)
        taken_table = (taken_ids[:, None] == lax.iota(jnp.int32, source_count)[None, :]).astype(
            jnp.bfloat16
        )
        picked = jnp.einsum(
            "gb,bqf->gqf", taken_table, source_blocks, preferred_element_type=jnp.float32
        ).astype(jnp.bfloat16)
        product = jnp.einsum(equation, tile_group, picked, preferred_element_type=jnp.float32)
        live_mask = first_slot + lax.iota(jnp.int32, group_size) < tile_total
        placed_table = (
            (placed_ids[:, None] == lax.iota(jnp.int32, target_blocks)[None, :])
            & live_mask[:, None]
        ).astype(jnp.float32)
        return total + jnp.einsum(
            "gt,gpf->tpf",
            placed_table,
            product,
            precision=lax.Precision.HIGHEST,
            preferred_element_type=jnp.float32,
        )

    total = jnp.zeros((target_blocks, block_rows, feature_width), jnp.float32)
    total = lax.fori_loop(0, capacity // group_size, group_step, total)
    return total.reshape(target_blocks * block_rows, feature_width)


def body(features, tile_values, tile_rows, tile_cols, tile_count, weight_in, weight_hidden):
    row_devices = lax.axis_size("row")
    col_devices = lax.axis_size("col")
    tile_total = tile_count[0]
    column_features = lax.all_gather(features, "row", axis=0, tiled=True)
    panel_terms = tile_products(
        tile_values, tile_cols, tile_rows, tile_total, column_features, col_devices, "gpq,gqf->gpf"
    )
    own_round = lax.psum_scatter(panel_terms, "col", scatter_dimension=0, tiled=True).astype(
        jnp.bfloat16
    )
    own_hidden = jax.nn.relu(
        jnp.dot(own_round, weight_in, preferred_element_type=jnp.float32)
    ).astype(jnp.bfloat16)
    hidden_rows = lax.all_gather(own_hidden, "col", axis=0, tiled=True)
    column_terms = tile_products(
        tile_values, tile_rows, tile_cols, tile_total, hidden_rows, row_devices, "gqp,gqf->gpf"
    )
    second_round = lax.psum_scatter(column_terms, "row", scatter_dimension=0, tiled=True).astype(
        jnp.bfloat16
    )
    return jax.nn.relu(
        jnp.dot(second_round, weight_hidden, preferred_element_type=jnp.float32)
    ).astype(jnp.bfloat16)


def solution(mesh):
    return jax.shard_map(
        body,
        mesh=mesh,
        in_specs=(
            P(("col", "row"), None),
            P(("row", "col"), None, None),
            P(("row", "col")),
            P(("row", "col")),
            P(("row", "col")),
            P(),
            P(),
        ),
        out_specs=P(("col", "row"), None),
        check_vma=False,
    )
```

profile of v0, /device:TPU:1, one launch (start us, length us, event | category | flops | bytes accessed | tf_op | source)
XLA Modules:
  0.0 753.5 jit_solution(3467903289357906287)
XLA Ops:
  6.5 16.2 %all_gather.6 = bf16[1024,128]{1,0:T(8,128)(2,1)S(1)} all-gather(bf16[128,128]{1,0:T(8,128)(2,1)} %param.11), channel_id=1, replica_groups=mesh['row'=8,'col'=32] {'row'}, dimensions={0}, use_global_device_ids=true | all-gather | bytes 294912 | tf_op jit(solution)/shard_map/all_gather | solution.py:49
  22.8 65.2 %while.28 = (s32[]{:T(128)}, f32[32,128,128]{2,0,1:T(8,128)}, s32[128]{0:T(128)}, s32[]{:T(128)}, bf16[128,128,128]{2,1,0:T(8,128)(2,1)}, /*index=5*/s32[128]{0:...) while((s32[]{:T(128)}, f32[32,128,128]{2,0,1:T(8,128)}, ...), condition=%wide.region_1.0_spmd.clone, body=%wide.region_0.0_spmd.clone.sunk | while | flops 173016224 | bytes 8127065 | solution.py:41
  23.9 1.3 fusion.57
  26.6 2.9 select_add_fusion.4
  30.6 1.3 fusion.57
  33.4 4.5 select_add_fusion.4
  41.7 4.5 select_add_fusion.4
  50.0 4.5 select_add_fusion.4
  55.7 1.3 fusion.57
  58.4 4.5 select_add_fusion.4
  64.0 1.3 fusion.57
  66.7 4.5 select_add_fusion.4
  72.3 1.3 fusion.57
  75.1 4.5 select_add_fusion.4
  80.7 1.3 fusion.57
  83.4 4.5 select_add_fusion.4
  88.0 4.2 copy.8
  92.2 211.7 %reduce-scatter.3.cloned.1.call-done = f32[128,128]{1,0:T(8,128)} async-done(((f32[4096,128]{1,0:T(8,128)}), f32[128,128]{1,0:T(8,128)}) %reduce-scatter.3.cloned.1.call-update) | async-done | bytes 65552 | tf_op jit(solution)/shard_map/reduce_scatter | solution.py:53
  304.0 1.8 fusion.31
  305.8 102.5 %all-gather.2.cloned.1.call-done = bf16[4096,1024]{1,0:T(8,128)(2,1)} async-done(((bf16[128,1024]{1,0:T(8,128)(2,1)}), bf16[4096,1024]{1,0:T(8,128)(2,1)}) %all-gather.2.cloned.1.call-update) | async-done | bytes 8388624 | tf_op jit(solution)/shard_map/all_gather | solution.py:59
  408.3 294.7 %while.29 = (s32[]{:T(128)}, f32[8,128,1024]{2,0,1:T(8,128)}, s32[128]{0:T(128)S(1)}, s32[]{:T(128)}, bf16[128,128,128]{2,1,0:T(8,128)(2,1)}, /*index=5*/s32[128...) while((s32[]{:T(128)}, f32[8,128,1024]{2,0,1:T(8,128)}, ...), condition=%wide.region_4.5_spmd.clone, body=%wide.region_3.4_spmd.clone.sunk | while | flops 874513152 | bytes 42467928 | solution.py:41
  408.4 12.4 %fusion.63 = bf16[16,128,1024]{2,0,1:T(8,128)(2,1)S(1)} fusion(bf16[32,128,1024]{2,1,0:T(8,128)(2,1)} %get-tuple-element.478, s32[16]{0:T(128)S(1)} %dynamic_slice.62), kind=kOutput, calls=%fused_computation.20.clone.1 | convolution fusion | flops 134218240 | bytes 12582976 | tf_op jit(solution)/shard_map/while/body/eval_jaxpr/gb,bqf->gqf/dot_general | solution.py:23
  420.7 9.6 %fusion.64 = f32[16,128,1024]{2,1,0:T(8,128)} fusion(bf16[16,128,1024]{2,0,1:T(8,128)(2,1)S(1)} %fusion.63, bf16[128,128,128]{2,1,0:T(8,128)(2,1)} %get-tuple-element.476, s32[]{:T(128)S(6)} %select_n.23), kind=kOutput, calls=%fused_computation.22.clone.1 | convolution fusion | flops 536870912 | bytes 13107204 | tf_op jit(solution)/shard_map/while/body/eval_jaxpr/gqp,gqf->gpf/dot_general | solution.py:26
  431.0 13.1 %select_add_fusion.5 = f32[8,128,1024]{2,0,1:T(8,128)} fusion(f32[8,128,1024]{2,0,1:T(8,128)} %get-tuple-element.462, f32[16,128,1024]{2,1,0:T(8,128)} %fusion.64, pred[]{:T(512)S(6)} %compare.7, s32[16]{0:T(128)S(1)} %dynamic_slice.63, pred[16]{0:T(512)(128)(4,1)S(1)} %add_compare_fusion.5), kind=kOutput, calls=%fused_computation.23.clone.1 | convolution fusion | flops 203424000 | bytes 16777296 | tf_op jit(solution)/shard_map/while/body/eval_jaxpr/gt,gpf->tpf/dot_general | solution.py:32
  444.2 12.4 %fusion.63 = bf16[16,128,1024]{2,0,1:T(8,128)(2,1)S(1)} fusion(bf16[32,128,1024]{2,1,0:T(8,128)(2,1)} %get-tuple-element.478, s32[16]{0:T(128)S(1)} %dynamic_slice.62), kind=kOutput, calls=%fused_computation.20.clone.1 | convolution fusion | flops 134218240 | bytes 12582976 | tf_op jit(solution)/shard_map/while/body/eval_jaxpr/gb,bqf->gqf/dot_general | solution.py:23
  456.5 9.6 %fusion.64 = f32[16,128,1024]{2,1,0:T(8,128)} fusion(bf16[16,128,1024]{2,0,1:T(8,128)(2,1)S(1)} %fusion.63, bf16[128,128,128]{2,1,0:T(8,128)(2,1)} %get-tuple-element.476, s32[]{:T(128)S(6)} %select_n.23), kind=kOutput, calls=%fused_computation.22.clone.1 | convolution fusion | flops 536870912 | bytes 13107204 | tf_op jit(solution)/shard_map/while/body/eval_jaxpr/gqp,gqf->gpf/dot_general | solution.py:26
  466.8 14.2 %select_add_fusion.5 = f32[8,128,1024]{2,0,1:T(8,128)} fusion(f32[8,128,1024]{2,0,1:T(8,128)} %get-tuple-element.462, f32[16,128,1024]{2,1,0:T(8,128)} %fusion.64, pred[]{:T(512)S(6)} %compare.7, s32[16]{0:T(128)S(1)} %dynamic_slice.63, pred[16]{0:T(512)(128)(4,1)S(1)} %add_compare_fusion.5), kind=kOutput, calls=%fused_computation.23.clone.1 | convolution fusion | flops 203424000 | bytes 16777296 | tf_op jit(solution)/shard_map/while/body/eval_jaxpr/gt,gpf->tpf/dot_general | solution.py:32
  481.2 12.4 %fusion.63 = bf16[16,128,1024]{2,0,1:T(8,128)(2,1)S(1)} fusion(bf16[32,128,1024]{2,1,0:T(8,128)(2,1)} %get-tuple-element.478, s32[16]{0:T(128)S(1)} %dynamic_slice.62), kind=kOutput, calls=%fused_computation.20.clone.1 | convolution fusion | flops 134218240 | bytes 12582976 | tf_op jit(solution)/shard_map/while/body/eval_jaxpr/gb,bqf->gqf/dot_general | solution.py:23
  493.5 9.6 %fusion.64 = f32[16,128,1024]{2,1,0:T(8,128)} fusion(bf16[16,128,1024]{2,0,1:T(8,128)(2,1)S(1)} %fusion.63, bf16[128,128,128]{2,1,0:T(8,128)(2,1)} %get-tuple-element.476, s32[]{:T(128)S(6)} %select_n.23), kind=kOutput, calls=%fused_computation.22.clone.1 | convolution fusion | flops 536870912 | bytes 13107204 | tf_op jit(solution)/shard_map/while/body/eval_jaxpr/gqp,gqf->gpf/dot_general | solution.py:26
  503.8 14.2 %select_add_fusion.5 = f32[8,128,1024]{2,0,1:T(8,128)} fusion(f32[8,128,1024]{2,0,1:T(8,128)} %get-tuple-element.462, f32[16,128,1024]{2,1,0:T(8,128)} %fusion.64, pred[]{:T(512)S(6)} %compare.7, s32[16]{0:T(128)S(1)} %dynamic_slice.63, pred[16]{0:T(512)(128)(4,1)S(1)} %add_compare_fusion.5), kind=kOutput, calls=%fused_computation.23.clone.1 | convolution fusion | flops 203424000 | bytes 16777296 | tf_op jit(solution)/shard_map/while/body/eval_jaxpr/gt,gpf->tpf/dot_general | solution.py:32
  518.1 12.4 %fusion.63 = bf16[16,128,1024]{2,0,1:T(8,128)(2,1)S(1)} fusion(bf16[32,128,1024]{2,1,0:T(8,128)(2,1)} %get-tuple-element.478, s32[16]{0:T(128)S(1)} %dynamic_slice.62), kind=kOutput, calls=%fused_computation.20.clone.1 | convolution fusion | flops 134218240 | bytes 12582976 | tf_op jit(solution)/shard_map/while/body/eval_jaxpr/gb,bqf->gqf/dot_general | solution.py:23
  530.5 9.6 %fusion.64 = f32[16,128,1024]{2,1,0:T(8,128)} fusion(bf16[16,128,1024]{2,0,1:T(8,128)(2,1)S(1)} %fusion.63, bf16[128,128,128]{2,1,0:T(8,128)(2,1)} %get-tuple-element.476, s32[]{:T(128)S(6)} %select_n.23), kind=kOutput, calls=%fused_computation.22.clone.1 | convolution fusion | flops 536870912 | bytes 13107204 | tf_op jit(solution)/shard_map/while/body/eval_jaxpr/gqp,gqf->gpf/dot_general | solution.py:26
  540.8 14.2 %select_add_fusion.5 = f32[8,128,1024]{2,0,1:T(8,128)} fusion(f32[8,128,1024]{2,0,1:T(8,128)} %get-tuple-element.462, f32[16,128,1024]{2,1,0:T(8,128)} %fusion.64, pred[]{:T(512)S(6)} %compare.7, s32[16]{0:T(128)S(1)} %dynamic_slice.63, pred[16]{0:T(512)(128)(4,1)S(1)} %add_compare_fusion.5), kind=kOutput, calls=%fused_computation.23.clone.1 | convolution fusion | flops 203424000 | bytes 16777296 | tf_op jit(solution)/shard_map/while/body/eval_jaxpr/gt,gpf->tpf/dot_general | solution.py:32
  555.1 12.4 %fusion.63 = bf16[16,128,1024]{2,0,1:T(8,128)(2,1)S(1)} fusion(bf16[32,128,1024]{2,1,0:T(8,128)(2,1)} %get-tuple-element.478, s32[16]{0:T(128)S(1)} %dynamic_slice.62), kind=kOutput, calls=%fused_computation.20.clone.1 | convolution fusion | flops 134218240 | bytes 12582976 | tf_op jit(solution)/shard_map/while/body/eval_jaxpr/gb,bqf->gqf/dot_general | solution.py:23
  567.5 9.6 %fusion.64 = f32[16,128,1024]{2,1,0:T(8,128)} fusion(bf16[16,128,1024]{2,0,1:T(8,128)(2,1)S(1)} %fusion.63, bf16[128,128,128]{2,1,0:T(8,128)(2,1)} %get-tuple-element.476, s32[]{:T(128)S(6)} %select_n.23), kind=kOutput, calls=%fused_computation.22.clone.1 | convolution fusion | flops 536870912 | bytes 13107204 | tf_op jit(solution)/shard_map/while/body/eval_jaxpr/gqp,gqf->gpf/dot_general | solution.py:26
  577.8 14.2 %select_add_fusion.5 = f32[8,128,1024]{2,0,1:T(8,128)} fusion(f32[8,128,1024]{2,0,1:T(8,128)} %get-tuple-element.462, f32[16,128,1024]{2,1,0:T(8,128)} %fusion.64, pred[]{:T(512)S(6)} %compare.7, s32[16]{0:T(128)S(1)} %dynamic_slice.63, pred[16]{0:T(512)(128)(4,1)S(1)} %add_compare_fusion.5), kind=kOutput, calls=%fused_computation.23.clone.1 | convolution fusion | flops 203424000 | bytes 16777296 | tf_op jit(solution)/shard_map/while/body/eval_jaxpr/gt,gpf->tpf/dot_general | solution.py:32
  592.1 12.4 %fusion.63 = bf16[16,128,1024]{2,0,1:T(8,128)(2,1)S(1)} fusion(bf16[32,128,1024]{2,1,0:T(8,128)(2,1)} %get-tuple-element.478, s32[16]{0:T(128)S(1)} %dynamic_slice.62), kind=kOutput, calls=%fused_computation.20.clone.1 | convolution fusion | flops 134218240 | bytes 12582976 | tf_op jit(solution)/shard_map/while/body/eval_jaxpr/gb,bqf->gqf/dot_general | solution.py:23
  604.5 9.6 %fusion.64 = f32[16,128,1024]{2,1,0:T(8,128)} fusion(bf16[16,128,1024]{2,0,1:T(8,128)(2,1)S(1)} %fusion.63, bf16[128,128,128]{2,1,0:T(8,128)(2,1)} %get-tuple-element.476, s32[]{:T(128)S(6)} %select_n.23), kind=kOutput, calls=%fused_computation.22.clone.1 | convolution fusion | flops 536870912 | bytes 13107204 | tf_op jit(solution)/shard_map/while/body/eval_jaxpr/gqp,gqf->gpf/dot_general | solution.py:26
  614.8 14.2 %select_add_fusion.5 = f32[8,128,1024]{2,0,1:T(8,128)} fusion(f32[8,128,1024]{2,0,1:T(8,128)} %get-tuple-element.462, f32[16,128,1024]{2,1,0:T(8,128)} %fusion.64, pred[]{:T(512)S(6)} %compare.7, s32[16]{0:T(128)S(1)} %dynamic_slice.63, pred[16]{0:T(512)(128)(4,1)S(1)} %add_compare_fusion.5), kind=kOutput, calls=%fused_computation.23.clone.1 | convolution fusion | flops 203424000 | bytes 16777296 | tf_op jit(solution)/shard_map/while/body/eval_jaxpr/gt,gpf->tpf/dot_general | solution.py:32
  629.1 12.4 %fusion.63 = bf16[16,128,1024]{2,0,1:T(8,128)(2,1)S(1)} fusion(bf16[32,128,1024]{2,1,0:T(8,128)(2,1)} %get-tuple-element.478, s32[16]{0:T(128)S(1)} %dynamic_slice.62), kind=kOutput, calls=%fused_computation.20.clone.1 | convolution fusion | flops 134218240 | bytes 12582976 | tf_op jit(solution)/shard_map/while/body/eval_jaxpr/gb,bqf->gqf/dot_general | solution.py:23
  641.5 9.6 %fusion.64 = f32[16,128,1024]{2,1,0:T(8,128)} fusion(bf16[16,128,1024]{2,0,1:T(8,128)(2,1)S(1)} %fusion.63, bf16[128,128,128]{2,1,0:T(8,128)(2,1)} %get-tuple-element.476, s32[]{:T(128)S(6)} %select_n.23), kind=kOutput, calls=%fused_computation.22.clone.1 | convolution fusion | flops 536870912 | bytes 13107204 | tf_op jit(solution)/shard_map/while/body/eval_jaxpr/gqp,gqf->gpf/dot_general | solution.py:26
  651.8 14.2 %select_add_fusion.5 = f32[8,128,1024]{2,0,1:T(8,128)} fusion(f32[8,128,1024]{2,0,1:T(8,128)} %get-tuple-element.462, f32[16,128,1024]{2,1,0:T(8,128)} %fusion.64, pred[]{:T(512)S(6)} %compare.7, s32[16]{0:T(128)S(1)} %dynamic_slice.63, pred[16]{0:T(512)(128)(4,1)S(1)} %add_compare_fusion.5), kind=kOutput, calls=%fused_computation.23.clone.1 | convolution fusion | flops 203424000 | bytes 16777296 | tf_op jit(solution)/shard_map/while/body/eval_jaxpr/gt,gpf->tpf/dot_general | solution.py:32
  666.1 12.4 %fusion.63 = bf16[16,128,1024]{2,0,1:T(8,128)(2,1)S(1)} fusion(bf16[32,128,1024]{2,1,0:T(8,128)(2,1)} %get-tuple-element.478, s32[16]{0:T(128)S(1)} %dynamic_slice.62), kind=kOutput, calls=%fused_computation.20.clone.1 | convolution fusion | flops 134218240 | bytes 12582976 | tf_op jit(solution)/shard_map/while/body/eval_jaxpr/gb,bqf->gqf/dot_general | solution.py:23
  678.5 9.6 %fusion.64 = f32[16,128,1024]{2,1,0:T(8,128)} fusion(bf16[16,128,1024]{2,0,1:T(8,128)(2,1)S(1)} %fusion.63, bf16[128,128,128]{2,1,0:T(8,128)(2,1)} %get-tuple-element.476, s32[]{:T(128)S(6)} %select_n.23), kind=kOutput, calls=%fused_computation.22.clone.1 | convolution fusion | flops 536870912 | bytes 13107204 | tf_op jit(solution)/shard_map/while/body/eval_jaxpr/gqp,gqf->gpf/dot_general | solution.py:26
  688.8 14.2 %select_add_fusion.5 = f32[8,128,1024]{2,0,1:T(8,128)} fusion(f32[8,128,1024]{2,0,1:T(8,128)} %get-tuple-element.462, f32[16,128,1024]{2,1,0:T(8,128)} %fusion.64, pred[]{:T(512)S(6)} %compare.7, s32[16]{0:T(128)S(1)} %dynamic_slice.63, pred[16]{0:T(512)(128)(4,1)S(1)} %add_compare_fusion.5), kind=kOutput, calls=%fused_computation.23.clone.1 | convolution fusion | flops 203424000 | bytes 16777296 | tf_op jit(solution)/shard_map/while/body/eval_jaxpr/gt,gpf->tpf/dot_general | solution.py:32
  703.0 6.6 copy.9
  709.6 35.1 %reduce-scatter.5.cloned.1.call-done = f32[128,1024]{1,0:T(8,128)} async-done(((f32[1024,1024]{1,0:T(8,128)}), f32[128,1024]{1,0:T(8,128)}) %reduce-scatter.5.cloned.1.call-update) | async-done | bytes 524304 | tf_op jit(solution)/shard_map/reduce_scatter | solution.py:63
  744.7 2.2 fusion.32
  (74 shorter events, 28.9 us)
Async XLA Ops:
  6.5 738.2 %copy-start = (bf16[1024,1024]{1,0:T(8,128)(2,1)S(1)}, bf16[1024,1024]{1,0:T(8,128)(2,1)}, u32[]{:S(2)}) copy-start(bf16[1024,1024]{1,0:T(8,128)(2,1)} %param.17) | copy-start | bytes 6291460
  6.5 297.4 %reduce-scatter.3.cloned.1.call-start = ((), (), s32[]{:S(2)}) async-start(), calls=%async_computation.2 | async-start | bytes 2162688 | tf_op jit(solution)/shard_map/reduce_scatter | solution.py:53
  87.9 216.0 %copy-start.1 = (bf16[128,1024]{1,0:T(8,128)(2,1)S(1)}, bf16[128,1024]{1,0:T(8,128)(2,1)}, u32[]{:S(2)}) copy-start(bf16[128,1024]{1,0:T(8,128)(2,1)} %param.16) | copy-start | bytes 786436
  87.9 320.3 %copy-start.2 = (s32[128]{0:T(128)S(1)}, s32[128]{0:T(128)}, u32[]{:S(2)}) copy-start(s32[128]{0:T(128)} %get-tuple-element.496) | copy-start | bytes 1540
  88.0 320.3 %copy-start.3 = (s32[128]{0:T(128)S(1)}, s32[128]{0:T(128)}, u32[]{:S(2)}) copy-start(s32[128]{0:T(128)} %get-tuple-element.497) | copy-start | bytes 1540
  92.2 316.1 %all-gather.2.cloned.1.call-start = ((), (), s32[]{:S(2)}) async-start(), calls=%async_computation.3 | async-start | bytes 8650752 | tf_op jit(solution)/shard_map/all_gather | solution.py:59
  305.7 439.0 %reduce-scatter.5.cloned.1.call-start = ((), (), s32[]{:S(2)}) async-start(), calls=%async_computation.4 | async-start | bytes 4718592 | tf_op jit(solution)/shard_map/reduce_scatter | solution.py:63
Sparse Core Ops, SparseCore 0:
  92.3 211.6 reduce-scatter.2
  306.9 101.3 all-gather.1
  709.7 34.9 reduce-scatter.4
where the time goes:
time: 757 us; the launch traced here: 753 us
  waiting for transfers between devices  349 us (46%)
  matrix products  340 us (45%)
  local copies, waits for them, and re-layouts  23.6 us (3%)
  blocking collectives  16.2 us (2%)
  between operations  13.1 us (2%)
  other arithmetic  10.4 us (1%)
    reduce_scatter x1, waiting for transfers between devices, body(): lax.psum_scatter(panel_terms, 'col', scatter_dimension=0, tiled=True)  212 us
    dot_general x16, matrix products, group_step(): jnp.einsum('gt,gpf->tpf', placed_table, product, precision=lax.Precision....  147 us
    all_gather x1, waiting for transfers between devices, body(): hidden_rows = lax.all_gather(own_hidden, 'col', axis=0, tiled=True)  102 us
    dot_general x16, matrix products, group_step(): jnp.einsum('gb,bqf->gqf', taken_table, source_blocks, preferred_element_t...  102 us
    dot_general x16, matrix products, group_step(): jnp.einsum(equation, tile_group, picked, preferred_element_type=jnp.float32)  87.2 us
    reduce_scatter x1, waiting for transfers between devices, body(): lax.psum_scatter(column_terms, 'row', scatter_dimension=0, tiled=True)  35.1 us
    all_gather x1, blocking collectives, body(): column_features = lax.all_gather(features, 'row', axis=0, tiled=True)  16.2 us
  transfers between devices with their start and end apart: 3, of which 3 were waited for; matrix products, arithmetic and copies ran while one was open for 0% of the time, Pallas kernels for 0%

commit v1 on v0

v1 whole, which is shorter than its diff:
```python
import functools

import jax
import jax.numpy as jnp
from jax import lax
from jax.experimental import pallas as pl
from jax.experimental.pallas import tpu as pltpu
from jax.sharding import Mesh
from jax.sharding import PartitionSpec as P

NY, NC, NX, NH, NL = 4, 2, 4, 4, 2
NZ = NH * NL
BLOCK = 128
COLS = NY * NC
SIDE = NZ * BLOCK
GROUP = 16
BF = jnp.bfloat16
F32 = jnp.float32


def shift(value, axis, size, step):
    return lax.ppermute(value, axis, [(i, (i + step) % size) for i in range(size)])


def place_kernel(transposed, code, tiles, dense, held, sems):
    groups = held.shape[0] // GROUP

    def load(g):
        part = pl.ds(g * GROUP, GROUP)
        return pltpu.make_async_copy(tiles.at[part], held.at[part], sems.at[g])

    for g in range(groups):
        load(g).start()
    dense[...] = jnp.zeros_like(dense)
    for g in range(groups):
        load(g).wait()
        for slot in range(g * GROUP, (g + 1) * GROUP):
            word = code[slot]
            row_at = lax.shift_right_logical(word, 4) & (NX * NZ - 1)
            col_at = lax.shift_right_logical(word, 1) & (COLS - 1)
            tile = jnp.where((word & 1) == 1, held[slot], jnp.zeros((BLOCK, BLOCK), BF))
            rows = pl.ds(pl.multiple_of(row_at * BLOCK, BLOCK), BLOCK)
            cols = pl.ds(pl.multiple_of(col_at * BLOCK, BLOCK), BLOCK)
            if transposed:
                dense[cols, rows] = tile.T
            else:
                dense[rows, cols] = tile


def place(transposed, code, tiles):
    shape = (NX * SIDE, COLS * BLOCK)
    shape = shape[::-1] if transposed else shape
    return pl.pallas_call(
        functools.partial(place_kernel, transposed),
        in_specs=[
            pl.BlockSpec(memory_space=pltpu.SMEM),
            pl.BlockSpec(memory_space=pltpu.HBM),
        ],
        out_specs=pl.BlockSpec(memory_space=pltpu.VMEM),
        out_shape=jax.ShapeDtypeStruct(shape, BF),
        scratch_shapes=[
            pltpu.VMEM(tiles.shape, BF),
            pltpu.SemaphoreType.DMA((tiles.shape[0] // GROUP,)),
        ],
        compiler_params=pltpu.CompilerParams(vmem_limit_bytes=16 * 2**20),
        cost_estimate=pl.CostEstimate(flops=10**10, bytes_accessed=2**24, transcendentals=0),
        name="place_t" if transposed else "place",
    )(code, pltpu.with_memory_space_constraint(tiles, pltpu.HBM))


def slot_codes(rows, cols, count):
    y, core = lax.axis_index("y"), lax.axis_index("core")
    col_at = ((cols + core) % NC) * NY + (cols // NC - y + NY) % NY
    live = lax.iota(jnp.int32, rows.shape[0]) < count[0]
    low = col_at * 2 + live
    x, z = rows // NZ, rows % NZ
    high, deep = z // NL, z % NL
    sent_at = (x * NL + deep) * NH + (high - lax.axis_index("zh") + NH) % NH
    far = (x - lax.axis_index("x") + NX) % NX
    held_at = jnp.where(far < 2, far, 5 - far) * NZ + z
    return (sent_at * 16 + low).astype(jnp.int32), (held_at * 16 + low).astype(jnp.int32)


def body(features, tile_values, tile_rows, tile_cols, tile_count, weight_in, weight_hidden):
    code, code_t = slot_codes(tile_rows, tile_cols, tile_count)

    pair = jnp.concatenate([features, shift(features, "core", NC, 1)], 0)
    after = {i: shift(pair, "y", NY, (NY - i) % NY) for i in (2, 1, 3)}
    code, after[2] = lax.optimization_barrier((code, after[2]))
    dense = place(False, code, tile_values)
    dense, after[1], after[3] = lax.optimization_barrier((dense, after[1], after[3]))
    near = [pair, after[1], after[2], after[3]]
    column = jnp.concatenate([p[:BLOCK] for p in near] + [p[BLOCK:] for p in near], 0)

    terms = jnp.dot(dense, column, preferred_element_type=F32).astype(BF)
    swapped = lax.all_to_all(terms, ("x", "zl"), 0, 0, tiled=True)
    total = swapped.reshape(NX * NL, NH * BLOCK, -1).astype(F32).sum(0)
    sent = total.astype(BF)
    got = [shift(sent[i * BLOCK : (i + 1) * BLOCK], "zh", NH, i) for i in (2, 1, 3)]
    own = total[:BLOCK] + got[0].astype(F32) + got[1].astype(F32) + got[2].astype(F32)
    own = own.astype(BF)

    own_all = jnp.broadcast_to(own[None], (NZ,) + own.shape).reshape(SIDE, -1)
    near = lax.all_to_all(own_all, ("zh", "zl"), 0, 0, tiled=True)
    code_t, near = lax.optimization_barrier((code_t, near))
    dense_t = place(True, code_t, tile_values)

    def fetch(panel, i):
        return shift(panel, "x", NX, (NX - i) % NX)

    def hidden(panel):
        states = jax.nn.relu(jnp.dot(panel, weight_in, preferred_element_type=F32))
        return lax.optimization_barrier(states.astype(BF))

    def second(rows, cols, states):
        return jnp.dot(dense_t[rows, cols], states, preferred_element_type=F32)

    every = slice(None)
    middle = [fetch(near, 1), fetch(near, 3)]
    states, near = lax.optimization_barrier((hidden(near), near))
    last = fetch(near, 2)
    term = second(every, slice(0, SIDE), states)
    middle = jnp.concatenate(middle, 0)
    term, middle = lax.optimization_barrier((term, middle))
    terms = second(every, slice(SIDE, 3 * SIDE), hidden(middle))
    terms, last = lax.optimization_barrier((terms, last))
    last = hidden(last)
    half = NY * BLOCK
    upper, lower = slice(0, half), slice(half, 2 * half)
    tail = slice(3 * SIDE, 4 * SIDE)
    given = (term[lower] + terms[lower] + second(lower, tail, last)).astype(BF)
    kept = term[upper] + terms[upper] + second(upper, tail, last)
    sums = {}
    for i in (2, 1, 3, 0):
        rows = slice(i * BLOCK, (i + 1) * BLOCK)
        mine = kept[rows] + shift(given[rows], "core", NC, 1).astype(F32)
        sums[i] = shift(mine.astype(BF), "y", NY, i).astype(F32) if i else mine
    own = (sums[0] + sums[2] + sums[1] + sums[3]).astype(BF)
    out = jnp.dot(own, weight_hidden, preferred_element_type=F32)
    return jax.nn.relu(out).astype(BF)


def solution(mesh):
    grid = Mesh(mesh.devices.reshape(NY, NC, NX, NH, NL), ("y", "core", "x", "zh", "zl"))
    nodes, slots = ("x", "zh", "zl", "y", "core"), ("y", "core", "x", "zh", "zl")
    return jax.shard_map(
        body,
        mesh=grid,
        in_specs=(
            P(nodes, None),
            P(slots, None, None),
            P(slots),
            P(slots),
            P(slots),
            P(),
            P(),
        ),
        out_specs=P(nodes, None),
        check_vma=False,
    )
```

time: 757 us -> 107 us (0.14)
  matrix products: 340 us -> 15.6 us
  waiting for transfers between devices: 349 us -> 25.9 us
  starting transfers between devices: 0.09 us -> 35.1 us
  local copies, waits for them, and re-layouts: 23.6 us -> 1.68 us
  between operations: 13.1 us -> 0.92 us
  other arithmetic: 10.4 us -> 1.2 us
    dot_general x50 -> x9, matrix products: 340 us -> 15.6 us  [the longest x4 9.4 us: second(): return jnp.dot(dense_t[rows, cols], states, preferred_element_type=F32)]
    reduce_scatter x2 -> x0, waiting for transfers between devices: 247 us -> none  [the longest x1 212 us: body(): lax.psum_scatter(panel_terms, 'col', scatter_dimension=0, tiled=True)]
    all_gather x1 -> x0, waiting for transfers between devices: 102 us -> none  [body(): hidden_rows = lax.all_gather(own_hidden, 'col', axis=0, tiled=True)]
    ppermute x0 -> x17, starting transfers between devices: none -> 29.6 us  [shift(): lax.ppermute(value, axis, [(i, (i + step) % size) for i in range(size)])]
    all_to_all x0 -> x1, blocking collectives: none -> 19.3 us  [body(): swapped = lax.all_to_all(terms, ('x', 'zl'), 0, 0, tiled=True)]
    ppermute x0 -> x17, waiting for transfers between devices: none -> 16.5 us  [shift(): lax.ppermute(value, axis, [(i, (i + step) % size) for i in range(size)])]
    all_gather x1 -> x0, blocking collectives: 16.2 us -> none  [body(): column_features = lax.all_gather(features, 'row', axis=0, tiled=True)]
    dynamic_slice x32 -> x0, local copies, waits for them, and re-layouts: 12.9 us -> none  [the longest x16 6.46 us: group_step(): placed_ids = lax.dynamic_slice_in_dim(target_ids, first_slot, group_size, 0)]
  transfers between devices with their start and end apart: 3 -> 18, of which waited for: 3 -> 7; matrix products, arithmetic and copies ran while one was open for 0% -> 11% of each run, Pallas kernels for 0% -> 6%
where the time goes in v1:
time: 107 us; the launch traced here: 106 us
  starting transfers between devices  35.1 us (33%)
  waiting for transfers between devices  25.9 us (24%)
  blocking collectives  19.3 us (18%)
  matrix products  15.6 us (15%)
  Pallas kernels  6.36 us (6%)
  local copies, waits for them, and re-layouts  1.68 us (2%)
  other arithmetic  1.2 us (1%)
    ppermute x17, starting transfers between devices, shift(): lax.ppermute(value, axis, [(i, (i + step) % size) for i in range(size)])  29.6 us
    all_to_all x1, blocking collectives, body(): swapped = lax.all_to_all(terms, ('x', 'zl'), 0, 0, tiled=True)  19.3 us
    ppermute x17, waiting for transfers between devices, shift(): lax.ppermute(value, axis, [(i, (i + step) % size) for i in range(size)])  16.5 us
    all_to_all x1, waiting for transfers between devices, body(): near = lax.all_to_all(own_all, ('zh', 'zl'), 0, 0, tiled=True)  9.45 us
    dot_general x4, matrix products, second(): return jnp.dot(dense_t[rows, cols], states, preferred_element_type=F32)  9.4 us
    pallas_call x2, Pallas kernels, place(): pl.pallas_call(functools.partial(place_kernel, transposed), in_specs=[pl....  6.36 us
    all_to_all x1, starting transfers between devices, body(): near = lax.all_to_all(own_all, ('zh', 'zl'), 0, 0, tiled=True)  5.53 us
    dot_general x3, matrix products, hidden(): states = jax.nn.relu(jnp.dot(panel, weight_in, preferred_element_type=F32))  2.63 us
  transfers between devices with their start and end apart: 18, of which 7 were waited for; matrix products, arithmetic and copies ran while one was open for 11% of the time, Pallas kernels for 6%

profile of v1, /device:TPU:1, one launch (start us, length us, event | category | flops | bytes accessed | tf_op | source)
XLA Modules:
  0.0 106.2 jit_solution(6482102098771709231)
XLA Ops:
  0.0 3.2 %collective-permute-start = (bf16[128,128]{1,0:T(8,128)(2,1)}, bf16[128,128]{1,0:T(8,128)(2,1)S(1)}, u32[]{:S(2)}, u32[]{:S(2)}) collective-permute-start(bf16[128,128]{1,0:T(8,128)(2,1)} %param.7), channel_id=1, source_target_pairs={{0,32},{32,0},{1,33},{33,1},{2,34},{34,2},{3,35},{35,3},{4,36},{36... | collective-permute-start | bytes 98312 | tf_op jit(solution)/shard_map/ppermute | solution.py:22
  3.2 0.8 constant_dynamic-update-slice_fusion.3
  4.7 0.0 collective-permute-done
  4.7 1.3 %collective-permute-start.1 = (bf16[256,128]{1,0:T(8,128)(2,1)S(1)}, bf16[256,128]{1,0:T(8,128)(2,1)S(1)}, u32[]{:S(2)}, u32[]{:S(2)}) collective-permute-start(bf16[256,128]{1,0:T(8,128)(2,1)S(1)} %constant_dynamic-update-slice_fusion), channel_id=1, source_target_pairs={{0,128},{64,192},{128,0},{192,64},{1,129},{65,193},{129,1},{193,65... | collective-permute-start | bytes 196616 | tf_op jit(solution)/shard_map/ppermute | solution.py:22
  6.0 0.7 multiply_add_fusion
  6.7 0.5 collective-permute-start.3
  7.1 2.3 %collective-permute-start.2 = (bf16[256,128]{1,0:T(8,128)(2,1)S(1)}, bf16[256,128]{1,0:T(8,128)(2,1)S(1)}, u32[]{:S(2)}, u32[]{:S(2)}) collective-permute-start(bf16[256,128]{1,0:T(8,128)(2,1)S(1)} %constant_dynamic-update-slice_fusion), channel_id=1, source_target_pairs={{0,192},{64,0},{128,64},{192,128},{1,193},{65,1},{129,65},{193,129... | collective-permute-start | bytes 196616 | tf_op jit(solution)/shard_map/ppermute | solution.py:22
  9.4 0.4 collective-permute-done.1
  9.8 3.0 %place.1 = bf16[4096,1024]{1,0:T(8,128)(2,1)S(1)} custom-call(s32[128]{0:T(128)S(1)} %get-tuple-element.18.code, bf16[128,128,128]{2,1,0:T(8,128)(2,1)} %tiles.3), custom_call_target="tpu_custom_call" | custom-call | flops 10000000000 | bytes 16777216 | tf_op jit(solution)/shard_map/place/pallas_call | solution.py:53
  12.8 0.0 collective-permute-done.3
  12.8 0.0 collective-permute-done.2
  12.9 2.3 %convolution_convert_fusion = bf16[4096,128]{1,0:T(8,128)(2,1)S(1)} fusion(bf16[4096,1024]{1,0:T(8,128)(2,1)S(1)} %place.1, bf16[1024,128]{1,0:T(8,128)(2,1)S(1)} %slice_dynamic-update-slice_fusion), kind=kOutput, calls=%fused_computation.1 | convolution fusion | flops 1074266112 | bytes 9699328 | tf_op jit(solution)/shard_map/dot_general | solution.py:95
  15.3 0.0 copy-start.2
  15.3 0.0 copy-start.1
  15.3 19.3 %all_to_all.18 = bf16[8,512,128]{2,1,0:T(8,128)(2,1)S(1)} all-to-all(bf16[8,512,128]{2,1,0:T(8,128)(2,1)S(1)} %bitcast.21), channel_id=1, replica_groups=mesh['y'=4,'core'=2,'x'=4,'zh'=4,'zl'=2] {'x','zl'}, dimensions={0} | all-to-all | bytes 2097152 | tf_op jit(solution)/shard_map/all_to_all | solution.py:96
  34.6 0.1 convert_reduce_fusion
  34.8 6.1 %collective-permute-start.4 = (bf16[128,128]{1,0:T(8,128)(2,1)S(1)}, bf16[128,128]{1,0:T(8,128)(2,1)S(1)}, u32[]{:S(2)}, u32[]{:S(2)}) collective-permute-start(bf16[128,128]{1,0:T(8,128)(2,1)S(1)} %get-tuple-element.41), channel_id=1, source_target_pairs={{0,4},{2,6},{4,0},{6,2},{1,5},{3,7},{5,1},{7,3},{8,12},{10,14},{12... | collective-permute-start | bytes 98312 | tf_op jit(solution)/shard_map/ppermute | solution.py:22
  40.9 0.3 collective-permute-start.6
  41.2 2.1 %collective-permute-start.5 = (bf16[128,128]{1,0:T(8,128)(2,1)S(1)}, bf16[128,128]{1,0:T(8,128)(2,1)S(1)}, u32[]{:S(2)}, u32[]{:S(2)}) collective-permute-start(bf16[128,128]{1,0:T(8,128)(2,1)S(1)} %get-tuple-element.43), channel_id=1, source_target_pairs={{0,2},{2,4},{4,6},{6,0},{1,3},{3,5},{5,7},{7,1},{8,10},{10,12},{12... | collective-permute-start | bytes 98312 | tf_op jit(solution)/shard_map/ppermute | solution.py:22
  43.3 0.0 collective-permute-done.4
  43.3 2.1 %collective-permute-done.6 = bf16[128,128]{1,0:T(8,128)(2,1)S(1)} collective-permute-done((bf16[128,128]{1,0:T(8,128)(2,1)S(1)}, bf16[128,128]{1,0:T(8,128)(2,1)S(1)}, u32[]{:S(2)}, u32[]{:S(2)}) %collective-permute-start.6) | collective-permute-done | bytes 32800 | tf_op jit(solution)/shard_map/ppermute | solution.py:22
  45.4 1.0 collective-permute-done.5
  46.4 0.7 broadcast_in_dim.2
  47.1 5.5 %all-to-all-start.1 = ((bf16[8,128,128]{2,1,0:T(8,128)(2,1)}), bf16[8,128,128]{2,1,0:T(8,128)(2,1)S(1)}, u32[]{:S(2)}, u32[]{:S(2)}) async-start(bf16[8,128,128]{2,1,0:T(8,128)(2,1)} %broadcast_in_dim.2), calls=%async_computation.1 | async-start | bytes 524288 | tf_op jit(solution)/shard_map/all_to_all | solution.py:104
  52.7 9.4 %all-to-all-done.1 = bf16[8,128,128]{2,1,0:T(8,128)(2,1)S(1)} async-done(((bf16[8,128,128]{2,1,0:T(8,128)(2,1)}), bf16[8,128,128]{2,1,0:T(8,128)(2,1)S(1)}, u32[]{:S(2)}, u32[]{:S(2)}) %all-to-all-start.1) | async-done | bytes 262176 | tf_op jit(solution)/shard_map/all_to_all | solution.py:104
  62.1 2.7 %collective-permute-start.7 = (bf16[1024,128]{1,0:T(8,128)(2,1)S(1)}, bf16[1024,128]{1,0:T(8,128)(2,1)S(1)}, u32[]{:S(2)}, u32[]{:S(2)}) collective-permute-start(bf16[1024,128]{1,0:T(8,128)(2,1)S(1)} %bitcast.18), channel_id=1, source_target_pairs={{0,24},{8,0},{16,8},{24,16},{1,25},{9,1},{17,9},{25,17},{2,26},{10... | collective-permute-start | bytes 786440 | tf_op jit(solution)/shard_map/ppermute | solution.py:22
  64.8 0.7 maximum_convert_fusion.2
  65.5 0.3 collective-permute-start.9
  65.8 3.4 %place_t.1 = bf16[1024,4096]{1,0:T(8,128)(2,1)S(1)} custom-call(s32[128]{0:T(128)S(1)} %multiply_add_fusion.1.code, bf16[128,128,128]{2,1,0:T(8,128)(2,1)} %tiles.3), custom_call_target="tpu_custom_call" | custom-call | flops 10000000000 | bytes 16777216 | tf_op jit(solution)/shard_map/place_t/pallas_call | solution.py:53
  69.2 2.3 %fusion.2 = f32[1024,1024]{1,0:T(8,128)S(1)} fusion(bf16[1024,1024]{1,0:T(8,128)(2,1)S(1)} %maximum_convert_fusion.2, bf16[1024,4096]{1,0:T(8,128)(2,1)S(1)} %place_t.1), kind=kOutput, calls=%fused_computation.6 | convolution fusion | flops 2147483648 | bytes 8388608 | tf_op jit(solution)/shard_map/dot_general | solution.py:116
  71.6 0.0 collective-permute-done.8
  71.6 1.2 %maximum_convert_fusion = bf16[2048,1024]{1,0:T(8,128)(2,1)S(1)} fusion(bf16[2048,128]{1,0:T(8,128)(2,1)S(1)} %pad_maximum_fusion, bf16[128,1024]{1,0:T(8,128)(2,1)S(1)} %copy-done.1), kind=kOutput, calls=%fused_computation | convolution fusion | flops 541065216 | bytes 4980736 | tf_op jit(solution)/shard_map/dot_general | solution.py:112
  72.9 4.5 %fusion = f32[1024,1024]{1,0:T(8,128)S(1)} fusion(bf16[2048,1024]{1,0:T(8,128)(2,1)S(1)} %maximum_convert_fusion, bf16[1024,4096]{1,0:T(8,128)(2,1)S(1)} %place_t.1), kind=kOutput, calls=%fused_computation.2 | convolution fusion | flops 4294967296 | bytes 12582912 | tf_op jit(solution)/shard_map/dot_general | solution.py:116
  77.4 0.7 maximum_convert_fusion.1
  78.1 1.3 %add_convert_fusion = bf16[512,1024]{1,0:T(8,128)(2,1)S(1)} fusion(f32[1024,1024]{1,0:T(8,128)S(1)} %fusion, f32[1024,1024]{1,0:T(8,128)S(1)} %fusion.2, bf16[1024,1024]{1,0:T(8,128)(2,1)S(1)} %maximum_convert_fusion.1, bf16[1024,4096]{1,0:T(8,128)(2,1)S(1)} %place_t.1), kind=kOutput, calls=%fused_computation.8 | convolution fusion | flops 1075314688 | bytes 8388608 | tf_op jit(solution)/shard_map/dot_general | solution.py:116
  79.4 0.1 fusion.36
  79.4 7.8 %collective-permute-start.15 = (bf16[128,1024]{1,0:T(8,128)(2,1)S(1)}, bf16[128,1024]{1,0:T(8,128)(2,1)S(1)}, u32[]{:S(2)}, u32[]{:S(2)}) collective-permute-start(bf16[128,1024]{1,0:T(8,128)(2,1)S(1)} %get-tuple-element.38), channel_id=1, source_target_pairs={{0,32},{32,0},{1,33},{33,1},{2,34},{34,2},{3,35},{35,3},{4,36},{36... | collective-permute-start | bytes 786440 | tf_op jit(solution)/shard_map/ppermute | solution.py:22
  87.2 0.1 collective-permute-start.13
  87.3 0.4 collective-permute-start.11
  87.8 1.3 %add_add_fusion = f32[512,1024]{1,0:T(8,128)S(1)} fusion(f32[1024,1024]{1,0:T(8,128)S(1)} %fusion, f32[1024,1024]{1,0:T(8,128)S(1)} %fusion.2, bf16[1024,1024]{1,0:T(8,128)(2,1)S(1)} %maximum_convert_fusion.1, bf16[1024,4096]{1,0:T(8,128)(2,1)S(1)} %place_t.1), kind=kOutput, calls=%fused_computation.9 | convolution fusion | flops 1074790400 | bytes 9437184 | tf_op jit(solution)/shard_map/dot_general | solution.py:116
  89.0 0.2 collective-permute-start.10
  89.3 0.3 fusion.15
  89.5 0.1 collective-permute-start.12
  89.6 2.3 %collective-permute-start.16 = (bf16[128,1024]{1,0:T(8,128)(2,1)S(1)}, bf16[128,1024]{1,0:T(8,128)(2,1)S(1)}, u32[]{:S(2)}, u32[]{:S(2)}) collective-permute-start(bf16[128,1024]{1,0:T(8,128)(2,1)S(1)} %get-tuple-element.35), channel_id=1, source_target_pairs={{0,192},{64,0},{128,64},{192,128},{1,193},{65,1},{129,65},{193,129... | collective-permute-start | bytes 786440 | tf_op jit(solution)/shard_map/ppermute | solution.py:22
  92.0 6.7 %collective-permute-done.12 = bf16[128,1024]{1,0:T(8,128)(2,1)S(1)} collective-permute-done((bf16[128,1024]{1,0:T(8,128)(2,1)S(1)}, bf16[128,1024]{1,0:T(8,128)(2,1)S(1)}, u32[]{:S(2)}, u32[]{:S(2)}) %collective-permute-start.12) | collective-permute-done | bytes 262176 | tf_op jit(solution)/shard_map/ppermute | solution.py:22
  98.6 2.9 %collective-permute-done.16 = bf16[128,1024]{1,0:T(8,128)(2,1)S(1)} collective-permute-done((bf16[128,1024]{1,0:T(8,128)(2,1)S(1)}, bf16[128,1024]{1,0:T(8,128)(2,1)S(1)}, u32[]{:S(2)}, u32[]{:S(2)}) %collective-permute-start.16) | collective-permute-done | bytes 262176 | tf_op jit(solution)/shard_map/ppermute | solution.py:22
  101.5 3.5 %collective-permute-done.14 = bf16[128,1024]{1,0:T(8,128)(2,1)S(1)} collective-permute-done((bf16[128,1024]{1,0:T(8,128)(2,1)S(1)}, bf16[128,1024]{1,0:T(8,128)(2,1)S(1)}, u32[]{:S(2)}, u32[]{:S(2)}) %collective-permute-start.14) | collective-permute-done | bytes 262176 | tf_op jit(solution)/shard_map/ppermute | solution.py:22
  105.0 1.2 %fusion.4 = bf16[128,1024]{1,0:T(8,128)(2,1)} fusion(bf16[1024,1024]{1,0:T(8,128)(2,1)S(1)} %copy-done, f32[512,1024]{1,0:T(8,128)S(1)} %add_add_fusion, bf16[128,1024]{1,0:T(8,128)(2,1)S(1)} %collective-permute-done.16, bf16[128,1024]{1,0:T(8,128)(2,1)S(1)} %collective-permute-done.14, bf16[128,1024]{1,0:T(8,128)(2,1)S(1)} %collective-permute-done.12, ...), kind=kOutput, calls=%fused_computation.12 | convolution fusion | flops 269877248 | bytes 3932160 | tf_op jit(solution)/shard_map/dot_general | solution.py:139
  (25 shorter events, 0.2 us)
Async XLA Ops:
  0.0 105.0 %copy-start = (bf16[1024,1024]{1,0:T(8,128)(2,1)S(1)}, bf16[1024,1024]{1,0:T(8,128)(2,1)}, u32[]{:S(2)}) copy-start(bf16[1024,1024]{1,0:T(8,128)(2,1)} %param.13) | copy-start | bytes 6291460
  0.0 4.7 %collective-permute-start = (bf16[128,128]{1,0:T(8,128)(2,1)}, bf16[128,128]{1,0:T(8,128)(2,1)S(1)}, u32[]{:S(2)}, u32[]{:S(2)}) collective-permute-start(bf16[128,128]{1,0:T(8,128)(2,1)} %param.7), channel_id=1, source_target_pairs={{0,32},{32,0},{1,33},{33,1},{2,34},{34,2},{3,35},{35,3},{4,36},{36... | collective-permute-start | bytes 98312 | tf_op jit(solution)/shard_map/ppermute | solution.py:22
  4.7 5.1 %collective-permute-start.1 = (bf16[256,128]{1,0:T(8,128)(2,1)S(1)}, bf16[256,128]{1,0:T(8,128)(2,1)S(1)}, u32[]{:S(2)}, u32[]{:S(2)}) collective-permute-start(bf16[256,128]{1,0:T(8,128)(2,1)S(1)} %constant_dynamic-update-slice_fusion), channel_id=1, source_target_pairs={{0,128},{64,192},{128,0},{192,64},{1,129},{65,193},{129,1},{193,65... | collective-permute-start | bytes 196616 | tf_op jit(solution)/shard_map/ppermute | solution.py:22
  6.7 6.1 %collective-permute-start.3 = (bf16[256,128]{1,0:T(8,128)(2,1)S(1)}, bf16[256,128]{1,0:T(8,128)(2,1)S(1)}, u32[]{:S(2)}, u32[]{:S(2)}) collective-permute-start(bf16[256,128]{1,0:T(8,128)(2,1)S(1)} %constant_dynamic-update-slice_fusion), channel_id=1, source_target_pairs={{0,64},{64,128},{128,192},{192,0},{1,65},{65,129},{129,193},{193,1... | collective-permute-start | bytes 196616 | tf_op jit(solution)/shard_map/ppermute | solution.py:22
  7.1 5.7 %collective-permute-start.2 = (bf16[256,128]{1,0:T(8,128)(2,1)S(1)}, bf16[256,128]{1,0:T(8,128)(2,1)S(1)}, u32[]{:S(2)}, u32[]{:S(2)}) collective-permute-start(bf16[256,128]{1,0:T(8,128)(2,1)S(1)} %constant_dynamic-update-slice_fusion), channel_id=1, source_target_pairs={{0,192},{64,0},{128,64},{192,128},{1,193},{65,1},{129,65},{193,129... | collective-permute-start | bytes 196616 | tf_op jit(solution)/shard_map/ppermute | solution.py:22
  15.3 37.4 %copy-start.2 = (s32[128]{0:T(128)S(1)}, s32[128]{0:T(128)}, u32[]{:S(2)}) copy-start(s32[128]{0:T(128)} %param.9) | copy-start | bytes 1540
  15.3 49.5 %copy-start.1 = (bf16[128,1024]{1,0:T(8,128)(2,1)S(1)}, bf16[128,1024]{1,0:T(8,128)(2,1)}, u32[]{:S(2)}) copy-start(bf16[128,1024]{1,0:T(8,128)(2,1)} %param.12) | copy-start | bytes 786436
  34.8 8.5 %collective-permute-start.4 = (bf16[128,128]{1,0:T(8,128)(2,1)S(1)}, bf16[128,128]{1,0:T(8,128)(2,1)S(1)}, u32[]{:S(2)}, u32[]{:S(2)}) collective-permute-start(bf16[128,128]{1,0:T(8,128)(2,1)S(1)} %get-tuple-element.41), channel_id=1, source_target_pairs={{0,4},{2,6},{4,0},{6,2},{1,5},{3,7},{5,1},{7,3},{8,12},{10,14},{12... | collective-permute-start | bytes 98312 | tf_op jit(solution)/shard_map/ppermute | solution.py:22
  40.9 4.5 %collective-permute-start.6 = (bf16[128,128]{1,0:T(8,128)(2,1)S(1)}, bf16[128,128]{1,0:T(8,128)(2,1)S(1)}, u32[]{:S(2)}, u32[]{:S(2)}) collective-permute-start(bf16[128,128]{1,0:T(8,128)(2,1)S(1)} %get-tuple-element.42), channel_id=1, source_target_pairs={{0,6},{2,0},{4,2},{6,4},{1,7},{3,1},{5,3},{7,5},{8,14},{10,8},{12,... | collective-permute-start | bytes 98312 | tf_op jit(solution)/shard_map/ppermute | solution.py:22
  41.2 5.2 %collective-permute-start.5 = (bf16[128,128]{1,0:T(8,128)(2,1)S(1)}, bf16[128,128]{1,0:T(8,128)(2,1)S(1)}, u32[]{:S(2)}, u32[]{:S(2)}) collective-permute-start(bf16[128,128]{1,0:T(8,128)(2,1)S(1)} %get-tuple-element.43), channel_id=1, source_target_pairs={{0,2},{2,4},{4,6},{6,0},{1,3},{3,5},{5,7},{7,1},{8,10},{10,12},{12... | collective-permute-start | bytes 98312 | tf_op jit(solution)/shard_map/ppermute | solution.py:22
  47.1 15.0 %all-to-all-start.1 = ((bf16[8,128,128]{2,1,0:T(8,128)(2,1)}), bf16[8,128,128]{2,1,0:T(8,128)(2,1)S(1)}, u32[]{:S(2)}, u32[]{:S(2)}) async-start(bf16[8,128,128]{2,1,0:T(8,128)(2,1)} %broadcast_in_dim.2), calls=%async_computation.1 | async-start | bytes 524288 | tf_op jit(solution)/shard_map/all_to_all | solution.py:104
  62.1 9.4 %collective-permute-start.8 = (bf16[1024,128]{1,0:T(8,128)(2,1)S(1)}, bf16[1024,128]{1,0:T(8,128)(2,1)S(1)}, u32[]{:S(2)}, u32[]{:S(2)}) collective-permute-start(bf16[1024,128]{1,0:T(8,128)(2,1)S(1)} %bitcast.17), channel_id=1, source_target_pairs={{0,8},{8,16},{16,24},{24,0},{1,9},{9,17},{17,25},{25,1},{2,10},{10... | collective-permute-start | bytes 786440 | tf_op jit(solution)/shard_map/ppermute | solution.py:22
  62.1 9.4 %collective-permute-start.7 = (bf16[1024,128]{1,0:T(8,128)(2,1)S(1)}, bf16[1024,128]{1,0:T(8,128)(2,1)S(1)}, u32[]{:S(2)}, u32[]{:S(2)}) collective-permute-start(bf16[1024,128]{1,0:T(8,128)(2,1)S(1)} %bitcast.18), channel_id=1, source_target_pairs={{0,24},{8,0},{16,8},{24,16},{1,25},{9,1},{17,9},{25,17},{2,26},{10... | collective-permute-start | bytes 786440 | tf_op jit(solution)/shard_map/ppermute | solution.py:22
  65.5 11.8 %collective-permute-start.9 = (bf16[1024,128]{1,0:T(8,128)(2,1)S(1)}, bf16[1024,128]{1,0:T(8,128)(2,1)S(1)}, u32[]{:S(2)}, u32[]{:S(2)}) collective-permute-start(bf16[1024,128]{1,0:T(8,128)(2,1)S(1)} %bitcast.20), channel_id=1, source_target_pairs={{0,16},{8,24},{16,0},{24,8},{1,17},{9,25},{17,1},{25,9},{2,18},{10... | collective-permute-start | bytes 786440 | tf_op jit(solution)/shard_map/ppermute | solution.py:22
  79.4 9.8 %collective-permute-start.15 = (bf16[128,1024]{1,0:T(8,128)(2,1)S(1)}, bf16[128,1024]{1,0:T(8,128)(2,1)S(1)}, u32[]{:S(2)}, u32[]{:S(2)}) collective-permute-start(bf16[128,1024]{1,0:T(8,128)(2,1)S(1)} %get-tuple-element.38), channel_id=1, source_target_pairs={{0,32},{32,0},{1,33},{33,1},{2,34},{34,2},{3,35},{35,3},{4,36},{36... | collective-permute-start | bytes 786440 | tf_op jit(solution)/shard_map/ppermute | solution.py:22
  87.2 2.0 %collective-permute-start.13 = (bf16[128,1024]{1,0:T(8,128)(2,1)S(1)}, bf16[128,1024]{1,0:T(8,128)(2,1)S(1)}, u32[]{:S(2)}, u32[]{:S(2)}) collective-permute-start(bf16[128,1024]{1,0:T(8,128)(2,1)S(1)} %get-tuple-element.39), channel_id=1, source_target_pairs={{0,32},{32,0},{1,33},{33,1},{2,34},{34,2},{3,35},{35,3},{4,36},{36... | collective-permute-start | bytes 786440 | tf_op jit(solution)/shard_map/ppermute | solution.py:22
  87.3 1.9 %collective-permute-start.11 = (bf16[128,1024]{1,0:T(8,128)(2,1)S(1)}, bf16[128,1024]{1,0:T(8,128)(2,1)S(1)}, u32[]{:S(2)}, u32[]{:S(2)}) collective-permute-start(bf16[128,1024]{1,0:T(8,128)(2,1)S(1)} %get-tuple-element.40), channel_id=1, source_target_pairs={{0,32},{32,0},{1,33},{33,1},{2,34},{34,2},{3,35},{35,3},{4,36},{36... | collective-permute-start | bytes 786440 | tf_op jit(solution)/shard_map/ppermute | solution.py:22
  89.0 2.9 %collective-permute-start.10 = (bf16[128,1024]{1,0:T(8,128)(2,1)S(1)}, bf16[128,1024]{1,0:T(8,128)(2,1)S(1)}, u32[]{:S(2)}, u32[]{:S(2)}) collective-permute-start(bf16[128,1024]{1,0:T(8,128)(2,1)S(1)} %get-tuple-element.37), channel_id=1, source_target_pairs={{0,32},{32,0},{1,33},{33,1},{2,34},{34,2},{3,35},{35,3},{4,36},{36... | collective-permute-start | bytes 786440 | tf_op jit(solution)/shard_map/ppermute | solution.py:22
  89.5 9.1 %collective-permute-start.12 = (bf16[128,1024]{1,0:T(8,128)(2,1)S(1)}, bf16[128,1024]{1,0:T(8,128)(2,1)S(1)}, u32[]{:S(2)}, u32[]{:S(2)}) collective-permute-start(bf16[128,1024]{1,0:T(8,128)(2,1)S(1)} %get-tuple-element.34), channel_id=1, source_target_pairs={{0,128},{64,192},{128,0},{192,64},{1,129},{65,193},{129,1},{193,65... | collective-permute-start | bytes 786440 | tf_op jit(solution)/shard_map/ppermute | solution.py:22
  89.6 11.9 %collective-permute-start.16 = (bf16[128,1024]{1,0:T(8,128)(2,1)S(1)}, bf16[128,1024]{1,0:T(8,128)(2,1)S(1)}, u32[]{:S(2)}, u32[]{:S(2)}) collective-permute-start(bf16[128,1024]{1,0:T(8,128)(2,1)S(1)} %get-tuple-element.35), channel_id=1, source_target_pairs={{0,192},{64,0},{128,64},{192,128},{1,193},{65,1},{129,65},{193,129... | collective-permute-start | bytes 786440 | tf_op jit(solution)/shard_map/ppermute | solution.py:22
  92.0 13.0 %collective-permute-start.14 = (bf16[128,1024]{1,0:T(8,128)(2,1)S(1)}, bf16[128,1024]{1,0:T(8,128)(2,1)S(1)}, u32[]{:S(2)}, u32[]{:S(2)}) collective-permute-start(bf16[128,1024]{1,0:T(8,128)(2,1)S(1)} %get-tuple-element.36), channel_id=1, source_target_pairs={{0,64},{64,128},{128,192},{192,0},{1,65},{65,129},{129,193},{193,1... | collective-permute-start | bytes 786440 | tf_op jit(solution)/shard_map/ppermute | solution.py:22

commit v2 on v1

--- a/solution.py
+++ b/solution.py
@@ -36,8 +36,8 @@
         load(g).wait()
         for slot in range(g * GROUP, (g + 1) * GROUP):
             word = code[slot]
-            row_at = lax.shift_right_logical(word, 4) & (NX * NZ - 1)
-            col_at = lax.shift_right_logical(word, 1) & (COLS - 1)
+            row_at = lax.shift_right_logical(word, 12 if transposed else 7) & (NX * NZ - 1)
+            col_at = lax.shift_right_logical(word, 4 if transposed else 1) & (COLS - 1)
             tile = jnp.where((word & 1) == 1, held[slot], jnp.zeros((BLOCK, BLOCK), BF))
             rows = pl.ds(pl.multiple_of(row_at * BLOCK, BLOCK), BLOCK)
             cols = pl.ds(pl.multiple_of(col_at * BLOCK, BLOCK), BLOCK)
@@ -69,20 +69,23 @@
 
 
 def slot_codes(rows, cols, count):
-    y, core = lax.axis_index("y"), lax.axis_index("core")
-    col_at = ((cols + core) % NC) * NY + (cols // NC - y + NY) % NY
+    other = (cols + lax.axis_index("core")) % NC
+    off = (cols // NC - lax.axis_index("y") + NY) % NY
     live = lax.iota(jnp.int32, rows.shape[0]) < count[0]
-    low = col_at * 2 + live
     x, z = rows // NZ, rows % NZ
     high, deep = z // NL, z % NL
-    sent_at = (x * NL + deep) * NH + (high - lax.axis_index("zh") + NH) % NH
+    sent_at = (x * NL + deep) * NH + high
     far = (x - lax.axis_index("x") + NX) % NX
-    held_at = jnp.where(far < 2, far, 5 - far) * NZ + z
-    return (sent_at * 16 + low).astype(jnp.int32), (held_at * 16 + low).astype(jnp.int32)
+    z_at = (deep + lax.axis_index("zl")) % NL * NH + high
+    held_at = jnp.where(far < 2, far, 5 - far) * NZ + z_at
+    late = NC + (1 - other) * (NY - 1) + jnp.where(off == 0, 2, off // 2)
+    order = jnp.where(off == 2, 1 - other, late)
+    word = (held_at * (NX * NZ) + sent_at) * COLS + order
+    return ((word * COLS + other * NY + off) * 2 + live).astype(jnp.int32)
 
 
 def body(features, tile_values, tile_rows, tile_cols, tile_count, weight_in, weight_hidden):
-    code, code_t = slot_codes(tile_rows, tile_cols, tile_count)
+    code = slot_codes(tile_rows, tile_cols, tile_count)
 
     pair = jnp.concatenate([features, shift(features, "core", NC, 1)], 0)
     after = {i: shift(pair, "y", NY, (NY - i) % NY) for i in (2, 1, 3)}
@@ -94,16 +97,14 @@
 
     terms = jnp.dot(dense, column, preferred_element_type=F32).astype(BF)
     swapped = lax.all_to_all(terms, ("x", "zl"), 0, 0, tiled=True)
-    total = swapped.reshape(NX * NL, NH * BLOCK, -1).astype(F32).sum(0)
-    sent = total.astype(BF)
-    got = [shift(sent[i * BLOCK : (i + 1) * BLOCK], "zh", NH, i) for i in (2, 1, 3)]
-    own = total[:BLOCK] + got[0].astype(F32) + got[1].astype(F32) + got[2].astype(F32)
+    sent = swapped.reshape(NX * NL, NH * BLOCK, -1).astype(F32).sum(0).astype(BF)
+    got = {i: shift(sent, "zh", NH, i) for i in (1, 3, 2)}
+    code, got[2] = lax.optimization_barrier((code, got[2]))
+    dense_t = place(True, code, tile_values)
+    dense_t, got[1], got[3] = lax.optimization_barrier((dense_t, got[1], got[3]))
+    own = sent.astype(F32) + got[1].astype(F32) + got[3].astype(F32) + got[2].astype(F32)
     own = own.astype(BF)
-
-    own_all = jnp.broadcast_to(own[None], (NZ,) + own.shape).reshape(SIDE, -1)
-    near = lax.all_to_all(own_all, ("zh", "zl"), 0, 0, tiled=True)
-    code_t, near = lax.optimization_barrier((code_t, near))
-    dense_t = place(True, code_t, tile_values)
+    near = jnp.concatenate([own, shift(own, "zl", NL, 1)], 0)
 
     def fetch(panel, i):
         return shift(panel, "x", NX, (NX - i) % NX)
@@ -112,31 +113,42 @@
         states = jax.nn.relu(jnp.dot(panel, weight_in, preferred_element_type=F32))
         return lax.optimization_barrier(states.astype(BF))
 
-    def second(rows, cols, states):
+    def second(i, rows, states):
+        cols = slice(i * SIDE, (i + 1) * SIDE)
         return jnp.dot(dense_t[rows, cols], states, preferred_element_type=F32)
 
     every = slice(None)
-    middle = [fetch(near, 1), fetch(near, 3)]
+    one, three = fetch(near, 1), fetch(near, 3)
     states, near = lax.optimization_barrier((hidden(near), near))
-    last = fetch(near, 2)
-    term = second(every, slice(0, SIDE), states)
-    middle = jnp.concatenate(middle, 0)
-    term, middle = lax.optimization_barrier((term, middle))
-    terms = second(every, slice(SIDE, 3 * SIDE), hidden(middle))
-    terms, last = lax.optimization_barrier((terms, last))
-    last = hidden(last)
-    half = NY * BLOCK
-    upper, lower = slice(0, half), slice(half, 2 * half)
-    tail = slice(3 * SIDE, 4 * SIDE)
-    given = (term[lower] + terms[lower] + second(lower, tail, last)).astype(BF)
-    kept = term[upper] + terms[upper] + second(upper, tail, last)
-    sums = {}
-    for i in (2, 1, 3, 0):
-        rows = slice(i * BLOCK, (i + 1) * BLOCK)
-        mine = kept[rows] + shift(given[rows], "core", NC, 1).astype(F32)
-        sums[i] = shift(mine.astype(BF), "y", NY, i).astype(F32) if i else mine
-    own = (sums[0] + sums[2] + sums[1] + sums[3]).astype(BF)
-    out = jnp.dot(own, weight_hidden, preferred_element_type=F32)
+    term = second(0, every, states)
+    term, one = lax.optimization_barrier((term, one))
+    term, three = lax.optimization_barrier((term, three))
+    term1 = second(1, every, hidden(one))
+    halves = [fetch(one[: SIDE // 2], 1), fetch(three[SIDE // 2 :], 3)]
+    two = jnp.concatenate(halves, 0)
+    term3 = second(2, every, hidden(three))
+    term3, two = lax.optimization_barrier((term3, two))
+    two = hidden(two)
+
+    def final(start, count, states):
+        rows = slice(start * BLOCK, (start + count) * BLOCK)
+        return term[rows] + term1[rows] + term3[rows] + second(3, rows, states)
+
+    def swap(given):
+        return shift(given, "core", NC, 1).astype(F32)
+
+    opposite = final(0, NC, two)
+    sums = {2: (opposite[BLOCK:] + swap(opposite[:BLOCK].astype(BF))).astype(BF)}
+    given = final(NC, NY - 1, two).astype(BF)
+    two, given, sums[2] = lax.optimization_barrier((two, given, sums[2]))
+    kept = final(NC + NY - 1, NY - 1, two)
+    for place_at, i in enumerate((1, 3, 0)):
+        rows = slice(place_at * BLOCK, (place_at + 1) * BLOCK)
+        sums[i] = kept[rows] + swap(given[rows])
+    own = sums[0]
+    for i in (2, 1, 3):
+        own = own + shift(sums[i].astype(BF), "y", NY, i).astype(F32)
+    out = jnp.dot(own.astype(BF), weight_hidden, preferred_element_type=F32)
     return jax.nn.relu(out).astype(BF)
 
 

time: 107 us -> 97.5 us (0.911)
  starting transfers between devices: 35.1 us -> 28.7 us
  waiting for transfers between devices: 25.9 us -> 23.8 us
    all_to_all x1 -> x0, waiting for transfers between devices: 9.45 us -> none  [body(): near = lax.all_to_all(own_all, ('zh', 'zl'), 0, 0, tiled=True)]
    ppermute x17 -> x19, waiting for transfers between devices: 16.5 us -> 23.8 us  [shift(): lax.ppermute(value, axis, [(i, (i + step) % size) for i in range(size)])]
    all_to_all x1 -> x0, starting transfers between devices: 5.53 us -> none  [body(): near = lax.all_to_all(own_all, ('zh', 'zl'), 0, 0, tiled=True)]
    ppermute x17 -> x19, starting transfers between devices: 29.6 us -> 28.7 us  [shift(): lax.ppermute(value, axis, [(i, (i + step) % size) for i in range(size)])]
    dot_general x4 -> x6, matrix products: 9.4 us -> 9.79 us  [second(): return jnp.dot(dense_t[rows, cols], states, preferred_element_type=F32)]
    dot_general x3 -> x4, matrix products: 2.63 us -> 2.78 us  [hidden(): states = jax.nn.relu(jnp.dot(panel, weight_in, preferred_element_type=F32))]
  transfers between devices with their start and end apart: 18 -> 19, of which waited for: 7 -> 10; matrix products, arithmetic and copies ran while one was open for 11% -> 12% of each run, Pallas kernels for 6% -> 7%
where the time goes in v2:
time: 97.5 us; the launch traced here: 97.3 us
  starting transfers between devices  28.7 us (29%)
  waiting for transfers between devices  23.8 us (24%)
  blocking collectives  19.2 us (20%)
  matrix products  16.2 us (17%)
  Pallas kernels  6.37 us (7%)
  other arithmetic  1.16 us (1%)
    ppermute x19, starting transfers between devices, shift(): lax.ppermute(value, axis, [(i, (i + step) % size) for i in range(size)])  28.7 us
    ppermute x19, waiting for transfers between devices, shift(): lax.ppermute(value, axis, [(i, (i + step) % size) for i in range(size)])  23.8 us
    all_to_all x1, blocking collectives, body(): swapped = lax.all_to_all(terms, ('x', 'zl'), 0, 0, tiled=True)  19.2 us
    dot_general x6, matrix products, second(): return jnp.dot(dense_t[rows, cols], states, preferred_element_type=F32)  9.79 us
    pallas_call x2, Pallas kernels, place(): pl.pallas_call(functools.partial(place_kernel, transposed), in_specs=[pl....  6.37 us
    dot_general x4, matrix products, hidden(): states = jax.nn.relu(jnp.dot(panel, weight_in, preferred_element_type=F32))  2.78 us
    dot_general x1, matrix products, body(): terms = jnp.dot(dense, column, preferred_element_type=F32).astype(BF)  2.34 us
  transfers between devices with their start and end apart: 19, of which 10 were waited for; matrix products, arithmetic and copies ran while one was open for 12% of the time, Pallas kernels for 7%

profile of v2, /device:TPU:1, one launch (start us, length us, event | category | flops | bytes accessed | tf_op | source)
XLA Modules:
  0.0 97.3 jit_solution(308449375686925306)
XLA Ops:
  0.0 3.2 %collective-permute-start = (bf16[128,128]{1,0:T(8,128)(2,1)}, bf16[128,128]{1,0:T(8,128)(2,1)S(1)}, u32[]{:S(2)}, u32[]{:S(2)}) collective-permute-start(bf16[128,128]{1,0:T(8,128)(2,1)} %param.7), channel_id=1, source_target_pairs={{0,32},{32,0},{1,33},{33,1},{2,34},{34,2},{3,35},{35,3},{4,36},{36... | collective-permute-start | bytes 98312 | tf_op jit(solution)/shard_map/ppermute | solution.py:22
  3.2 0.8 constant_dynamic-update-slice_fusion.3
  4.7 1.3 %collective-permute-start.1 = (bf16[256,128]{1,0:T(8,128)(2,1)S(1)}, bf16[256,128]{1,0:T(8,128)(2,1)S(1)}, u32[]{:S(2)}, u32[]{:S(2)}) collective-permute-start(bf16[256,128]{1,0:T(8,128)(2,1)S(1)} %constant_dynamic-update-slice_fusion), channel_id=1, source_target_pairs={{0,128},{64,192},{128,0},{192,64},{1,129},{65,193},{129,1},{193,65... | collective-permute-start | bytes 196616 | tf_op jit(solution)/shard_map/ppermute | solution.py:22
  6.0 0.7 fusion.28.code
  6.7 0.5 collective-permute-start.3
  7.1 2.3 %collective-permute-start.2 = (bf16[256,128]{1,0:T(8,128)(2,1)S(1)}, bf16[256,128]{1,0:T(8,128)(2,1)S(1)}, u32[]{:S(2)}, u32[]{:S(2)}) collective-permute-start(bf16[256,128]{1,0:T(8,128)(2,1)S(1)} %constant_dynamic-update-slice_fusion), channel_id=1, source_target_pairs={{0,192},{64,0},{128,64},{192,128},{1,193},{65,1},{129,65},{193,129... | collective-permute-start | bytes 196616 | tf_op jit(solution)/shard_map/ppermute | solution.py:22
  9.4 0.4 collective-permute-done.1
  9.8 3.0 %place.1 = bf16[4096,1024]{1,0:T(8,128)(2,1)S(1)} custom-call(s32[128]{0:T(128)S(1)} %fusion.28.code, bf16[128,128,128]{2,1,0:T(8,128)(2,1)} %tiles.3), custom_call_target="tpu_custom_call" | custom-call | flops 10000000000 | bytes 16777216 | tf_op jit(solution)/shard_map/place/pallas_call | solution.py:53
  12.9 2.3 %convolution_convert_fusion = bf16[4096,128]{1,0:T(8,128)(2,1)S(1)} fusion(bf16[4096,1024]{1,0:T(8,128)(2,1)S(1)} %place.1, bf16[1024,128]{1,0:T(8,128)(2,1)S(1)} %slice_dynamic-update-slice_fusion), kind=kOutput, calls=%fused_computation | convolution fusion | flops 1074266112 | bytes 9699328 | tf_op jit(solution)/shard_map/dot_general | solution.py:98
  15.3 19.2 %all_to_all.9 = bf16[8,512,128]{2,1,0:T(8,128)(2,1)S(1)} all-to-all(bf16[8,512,128]{2,1,0:T(8,128)(2,1)S(1)} %bitcast.19), channel_id=1, replica_groups=mesh['y'=4,'core'=2,'x'=4,'zh'=4,'zl'=2] {'x','zl'}, dimensions={0} | all-to-all | bytes 2097152 | tf_op jit(solution)/shard_map/all_to_all | solution.py:99
  34.5 0.1 reduce_sum.12
  34.6 6.1 %collective-permute-start.4 = (bf16[512,128]{1,0:T(8,128)(2,1)S(1)}, bf16[512,128]{1,0:T(8,128)(2,1)S(1)}, u32[]{:S(2)}, u32[]{:S(2)}) collective-permute-start(bf16[512,128]{1,0:T(8,128)(2,1)S(1)} %reduce_sum.12), channel_id=1, source_target_pairs={{0,4},{2,6},{4,0},{6,2},{1,5},{3,7},{5,1},{7,3},{8,12},{10,14},{12... | collective-permute-start | bytes 393224 | tf_op jit(solution)/shard_map/ppermute | solution.py:22
  40.7 0.3 collective-permute-start.6
  41.0 2.1 %collective-permute-start.5 = (bf16[512,128]{1,0:T(8,128)(2,1)S(1)}, bf16[512,128]{1,0:T(8,128)(2,1)S(1)}, u32[]{:S(2)}, u32[]{:S(2)}) collective-permute-start(bf16[512,128]{1,0:T(8,128)(2,1)S(1)} %reduce_sum.12), channel_id=1, source_target_pairs={{0,2},{2,4},{4,6},{6,0},{1,3},{3,5},{5,7},{7,1},{8,10},{10,12},{12... | collective-permute-start | bytes 393224 | tf_op jit(solution)/shard_map/ppermute | solution.py:22
  43.1 0.1 collective-permute-done.4
  43.2 3.4 %place_t.1 = bf16[1024,4096]{1,0:T(8,128)(2,1)S(1)} custom-call(s32[128]{0:T(128)S(1)} %fusion.28.code, bf16[128,128,128]{2,1,0:T(8,128)(2,1)} %tiles.3), custom_call_target="tpu_custom_call" | custom-call | flops 10000000000 | bytes 16777216 | tf_op jit(solution)/shard_map/place_t/pallas_call | solution.py:53
  46.6 6.8 %collective-permute-done.6 = bf16[512,128]{1,0:T(8,128)(2,1)S(1)} collective-permute-done((bf16[512,128]{1,0:T(8,128)(2,1)S(1)}, bf16[512,128]{1,0:T(8,128)(2,1)S(1)}, u32[]{:S(2)}, u32[]{:S(2)}) %collective-permute-start.6) | collective-permute-done | bytes 131104 | tf_op jit(solution)/shard_map/ppermute | solution.py:22
  53.5 0.6 collective-permute-start.7
  54.2 3.9 %collective-permute-done.7 = bf16[512,128]{1,0:T(8,128)(2,1)S(1)} collective-permute-done((bf16[512,128]{1,0:T(8,128)(2,1)S(1)}, bf16[512,128]{1,0:T(8,128)(2,1)S(1)}, u32[]{:S(2)}, u32[]{:S(2)}) %collective-permute-start.7) | collective-permute-done | bytes 131104 | tf_op jit(solution)/shard_map/ppermute | solution.py:22
  58.1 1.5 %collective-permute-start.8 = (bf16[1024,128]{1,0:T(8,128)(2,1)S(1)}, bf16[1024,128]{1,0:T(8,128)(2,1)S(1)}, u32[]{:S(2)}, u32[]{:S(2)}) collective-permute-start(bf16[1024,128]{1,0:T(8,128)(2,1)S(1)} %pad_maximum_fusion), channel_id=1, source_target_pairs={{0,24},{8,0},{16,8},{24,16},{1,25},{9,1},{17,9},{25,17},{2,26},{10... | collective-permute-start | bytes 786440 | tf_op jit(solution)/shard_map/ppermute | solution.py:22
  59.6 0.2 collective-permute-start.9
  59.8 0.7 maximum_convert_fusion.3
  60.5 2.3 %fusion.4 = f32[1024,1024]{1,0:T(8,128)S(1)} fusion(bf16[1024,1024]{1,0:T(8,128)(2,1)S(1)} %maximum_convert_fusion.3, bf16[1024,4096]{1,0:T(8,128)(2,1)S(1)} %place_t.1), kind=kOutput, calls=%fused_computation.9 | convolution fusion | flops 2147483648 | bytes 8388608 | tf_op jit(solution)/shard_map/dot_general | solution.py:118
  62.9 1.9 %collective-permute-done.8 = bf16[1024,128]{1,0:T(8,128)(2,1)S(1)} collective-permute-done((bf16[1024,128]{1,0:T(8,128)(2,1)S(1)}, bf16[1024,128]{1,0:T(8,128)(2,1)S(1)}, u32[]{:S(2)}, u32[]{:S(2)}) %collective-permute-start.8) | collective-permute-done | bytes 262176 | tf_op jit(solution)/shard_map/ppermute | solution.py:22
  64.8 0.7 maximum_convert_fusion.2
  65.5 1.4 %collective-permute-done.9 = bf16[1024,128]{1,0:T(8,128)(2,1)S(1)} collective-permute-done((bf16[1024,128]{1,0:T(8,128)(2,1)S(1)}, bf16[1024,128]{1,0:T(8,128)(2,1)S(1)}, u32[]{:S(2)}, u32[]{:S(2)}) %collective-permute-start.9) | collective-permute-done | bytes 262176 | tf_op jit(solution)/shard_map/ppermute | solution.py:22
  66.9 0.7 maximum_convert_fusion.1
  67.6 1.1 %collective-permute-start.10 = (bf16[512,128]{1,0:T(8,128)(2,1)S(1)}, bf16[512,128]{1,0:T(8,128)(2,1)S(1)}, u32[]{:S(2)}, u32[]{:S(2)}) collective-permute-start(bf16[512,128]{1,0:T(8,128)(2,1)S(1)} %slice.105), channel_id=1, source_target_pairs={{0,24},{8,0},{16,8},{24,16},{1,25},{9,1},{17,9},{25,17},{2,26},{10... | collective-permute-start | bytes 393224 | tf_op jit(solution)/shard_map/ppermute | solution.py:22
  68.7 0.5 collective-permute-start.11
  69.2 2.3 %fusion.2 = f32[1024,1024]{1,0:T(8,128)S(1)} fusion(bf16[1024,1024]{1,0:T(8,128)(2,1)S(1)} %maximum_convert_fusion.2, bf16[1024,4096]{1,0:T(8,128)(2,1)S(1)} %place_t.1), kind=kOutput, calls=%fused_computation.7 | convolution fusion | flops 2147483648 | bytes 8388608 | tf_op jit(solution)/shard_map/dot_general | solution.py:118
  71.5 2.3 %fusion = f32[1024,1024]{1,0:T(8,128)S(1)} fusion(bf16[1024,1024]{1,0:T(8,128)(2,1)S(1)} %maximum_convert_fusion.1, bf16[1024,4096]{1,0:T(8,128)(2,1)S(1)} %place_t.1), kind=kOutput, calls=%fused_computation.5 | convolution fusion | flops 2147483648 | bytes 8388608 | tf_op jit(solution)/shard_map/dot_general | solution.py:118
  73.9 0.7 maximum_convert_fusion
  74.6 0.8 convolution_add_fusion
  75.4 3.9 %collective-permute-start.12 = (bf16[128,1024]{1,0:T(8,128)(2,1)S(1)}, bf16[128,1024]{1,0:T(8,128)(2,1)S(1)}, u32[]{:S(2)}, u32[]{:S(2)}) collective-permute-start(bf16[128,1024]{1,0:T(8,128)(2,1)S(1)} %slice.194), channel_id=1, source_target_pairs={{0,32},{32,0},{1,33},{33,1},{2,34},{34,2},{3,35},{35,3},{4,36},{36... | collective-permute-start | bytes 786440 | tf_op jit(solution)/shard_map/ppermute | solution.py:22
  79.4 1.0 %fusion.8 = bf16[384,1024]{1,0:T(8,128)(2,1)S(1)} fusion(f32[1024,1024]{1,0:T(8,128)S(1)} %fusion.2, f32[1024,1024]{1,0:T(8,128)S(1)} %fusion, f32[1024,1024]{1,0:T(8,128)S(1)} %fusion.4, bf16[1024,1024]{1,0:T(8,128)(2,1)S(1)} %maximum_convert_fusion, bf16[1024,4096]{1,0:T(8,128)(2,1)S(1)} %place_t.1), kind=kOutput, calls=%fused_computation.14 | convolution fusion | flops 806879232 | bytes 8388608 | tf_op jit(solution)/shard_map/dot_general | solution.py:118
  80.4 0.1 collective-permute-done.12
  80.6 1.1 %collective-permute-start.14 = (bf16[128,1024]{1,0:T(8,128)(2,1)S(1)}, bf16[128,1024]{1,0:T(8,128)(2,1)S(1)}, u32[]{:S(2)}, u32[]{:S(2)}) collective-permute-start(bf16[128,1024]{1,0:T(8,128)(2,1)S(1)} %fusion.21), channel_id=1, source_target_pairs={{0,128},{64,192},{128,0},{192,64},{1,129},{65,193},{129,1},{193,65... | collective-permute-start | bytes 786440 | tf_op jit(solution)/shard_map/ppermute | solution.py:22
  81.8 0.7 collective-permute-start.13
  82.5 0.1 collective-permute-start.17
  82.6 0.4 collective-permute-start.15
  83.0 1.0 %fusion.10 = f32[384,1024]{1,0:T(8,128)S(1)} fusion(f32[1024,1024]{1,0:T(8,128)S(1)} %fusion.2, f32[1024,1024]{1,0:T(8,128)S(1)} %fusion, f32[1024,1024]{1,0:T(8,128)S(1)} %fusion.4, bf16[1024,1024]{1,0:T(8,128)(2,1)S(1)} %maximum_convert_fusion, bf16[1024,4096]{1,0:T(8,128)(2,1)S(1)} %place_t.1), kind=kOutput, calls=%fused_computation.17 | convolution fusion | flops 806486016 | bytes 9175040 | tf_op jit(solution)/shard_map/dot_general | solution.py:118
  84.1 0.4 collective-permute-done.15
  84.4 0.1 fusion.16
  84.6 0.1 collective-permute-start.16
  84.7 2.7 %collective-permute-start.18 = (bf16[128,1024]{1,0:T(8,128)(2,1)S(1)}, bf16[128,1024]{1,0:T(8,128)(2,1)S(1)}, u32[]{:S(2)}, u32[]{:S(2)}) collective-permute-start(bf16[128,1024]{1,0:T(8,128)(2,1)S(1)} %get-tuple-element.46), channel_id=1, source_target_pairs={{0,192},{64,0},{128,64},{192,128},{1,193},{65,1},{129,65},{193,129... | collective-permute-start | bytes 786440 | tf_op jit(solution)/shard_map/ppermute | solution.py:22
  87.3 2.3 %collective-permute-done.14 = bf16[128,1024]{1,0:T(8,128)(2,1)S(1)} collective-permute-done((bf16[128,1024]{1,0:T(8,128)(2,1)S(1)}, bf16[128,1024]{1,0:T(8,128)(2,1)S(1)}, u32[]{:S(2)}, u32[]{:S(2)}) %collective-permute-start.14) | collective-permute-done | bytes 262176 | tf_op jit(solution)/shard_map/ppermute | solution.py:22
  89.7 6.3 %collective-permute-done.16 = bf16[128,1024]{1,0:T(8,128)(2,1)S(1)} collective-permute-done((bf16[128,1024]{1,0:T(8,128)(2,1)S(1)}, bf16[128,1024]{1,0:T(8,128)(2,1)S(1)}, u32[]{:S(2)}, u32[]{:S(2)}) %collective-permute-start.16) | collective-permute-done | bytes 262176 | tf_op jit(solution)/shard_map/ppermute | solution.py:22
  96.0 1.2 %fusion.11 = bf16[128,1024]{1,0:T(8,128)(2,1)} fusion(bf16[1024,1024]{1,0:T(8,128)(2,1)S(1)} %copy-done, f32[384,1024]{1,0:T(8,128)S(1)} %fusion.10, bf16[128,1024]{1,0:T(8,128)(2,1)S(1)} %collective-permute-done.18, bf16[128,1024]{1,0:T(8,128)(2,1)S(1)} %collective-permute-done.16, bf16[128,1024]{1,0:T(8,128)(2,1)S(1)} %collective-permute-done.14, ...), kind=kOutput, calls=%fused_computation.20 | convolution fusion | flops 269877248 | bytes 3932160 | tf_op jit(solution)/shard_map/dot_general | solution.py:151
  (29 shorter events, 0.4 us)
Async XLA Ops:
  0.0 96.0 %copy-start = (bf16[1024,1024]{1,0:T(8,128)(2,1)S(1)}, bf16[1024,1024]{1,0:T(8,128)(2,1)}, u32[]{:S(2)}) copy-start(bf16[1024,1024]{1,0:T(8,128)(2,1)} %param.13) | copy-start | bytes 6291460
  0.0 4.7 %collective-permute-start = (bf16[128,128]{1,0:T(8,128)(2,1)}, bf16[128,128]{1,0:T(8,128)(2,1)S(1)}, u32[]{:S(2)}, u32[]{:S(2)}) collective-permute-start(bf16[128,128]{1,0:T(8,128)(2,1)} %param.7), channel_id=1, source_target_pairs={{0,32},{32,0},{1,33},{33,1},{2,34},{34,2},{3,35},{35,3},{4,36},{36... | collective-permute-start | bytes 98312 | tf_op jit(solution)/shard_map/ppermute | solution.py:22
  4.7 5.1 %collective-permute-start.1 = (bf16[256,128]{1,0:T(8,128)(2,1)S(1)}, bf16[256,128]{1,0:T(8,128)(2,1)S(1)}, u32[]{:S(2)}, u32[]{:S(2)}) collective-permute-start(bf16[256,128]{1,0:T(8,128)(2,1)S(1)} %constant_dynamic-update-slice_fusion), channel_id=1, source_target_pairs={{0,128},{64,192},{128,0},{192,64},{1,129},{65,193},{129,1},{193,65... | collective-permute-start | bytes 196616 | tf_op jit(solution)/shard_map/ppermute | solution.py:22
  6.7 6.1 %collective-permute-start.3 = (bf16[256,128]{1,0:T(8,128)(2,1)S(1)}, bf16[256,128]{1,0:T(8,128)(2,1)S(1)}, u32[]{:S(2)}, u32[]{:S(2)}) collective-permute-start(bf16[256,128]{1,0:T(8,128)(2,1)S(1)} %constant_dynamic-update-slice_fusion), channel_id=1, source_target_pairs={{0,64},{64,128},{128,192},{192,0},{1,65},{65,129},{129,193},{193,1... | collective-permute-start | bytes 196616 | tf_op jit(solution)/shard_map/ppermute | solution.py:22
  7.1 5.7 %collective-permute-start.2 = (bf16[256,128]{1,0:T(8,128)(2,1)S(1)}, bf16[256,128]{1,0:T(8,128)(2,1)S(1)}, u32[]{:S(2)}, u32[]{:S(2)}) collective-permute-start(bf16[256,128]{1,0:T(8,128)(2,1)S(1)} %constant_dynamic-update-slice_fusion), channel_id=1, source_target_pairs={{0,192},{64,0},{128,64},{192,128},{1,193},{65,1},{129,65},{193,129... | collective-permute-start | bytes 196616 | tf_op jit(solution)/shard_map/ppermute | solution.py:22
  34.6 25.2 %copy-start.1 = (bf16[128,1024]{1,0:T(8,128)(2,1)S(1)}, bf16[128,1024]{1,0:T(8,128)(2,1)}, u32[]{:S(2)}) copy-start(bf16[128,1024]{1,0:T(8,128)(2,1)} %param.12) | copy-start | bytes 786436
  34.6 8.6 %collective-permute-start.4 = (bf16[512,128]{1,0:T(8,128)(2,1)S(1)}, bf16[512,128]{1,0:T(8,128)(2,1)S(1)}, u32[]{:S(2)}, u32[]{:S(2)}) collective-permute-start(bf16[512,128]{1,0:T(8,128)(2,1)S(1)} %reduce_sum.12), channel_id=1, source_target_pairs={{0,4},{2,6},{4,0},{6,2},{1,5},{3,7},{5,1},{7,3},{8,12},{10,14},{12... | collective-permute-start | bytes 393224 | tf_op jit(solution)/shard_map/ppermute | solution.py:22
  40.7 12.7 %collective-permute-start.6 = (bf16[512,128]{1,0:T(8,128)(2,1)S(1)}, bf16[512,128]{1,0:T(8,128)(2,1)S(1)}, u32[]{:S(2)}, u32[]{:S(2)}) collective-permute-start(bf16[512,128]{1,0:T(8,128)(2,1)S(1)} %reduce_sum.12), channel_id=1, source_target_pairs={{0,6},{2,0},{4,2},{6,4},{1,7},{3,1},{5,3},{7,5},{8,14},{10,8},{12,... | collective-permute-start | bytes 393224 | tf_op jit(solution)/shard_map/ppermute | solution.py:22
  41.0 12.4 %collective-permute-start.5 = (bf16[512,128]{1,0:T(8,128)(2,1)S(1)}, bf16[512,128]{1,0:T(8,128)(2,1)S(1)}, u32[]{:S(2)}, u32[]{:S(2)}) collective-permute-start(bf16[512,128]{1,0:T(8,128)(2,1)S(1)} %reduce_sum.12), channel_id=1, source_target_pairs={{0,2},{2,4},{4,6},{6,0},{1,3},{3,5},{5,7},{7,1},{8,10},{10,12},{12... | collective-permute-start | bytes 393224 | tf_op jit(solution)/shard_map/ppermute | solution.py:22
  53.5 4.6 %collective-permute-start.7 = (bf16[512,128]{1,0:T(8,128)(2,1)S(1)}, bf16[512,128]{1,0:T(8,128)(2,1)S(1)}, u32[]{:S(2)}, u32[]{:S(2)}) collective-permute-start(bf16[512,128]{1,0:T(8,128)(2,1)S(1)} %add_convert_fusion), channel_id=1, source_target_pairs={{0,1},{1,0},{2,3},{3,2},{4,5},{5,4},{6,7},{7,6},{8,9},{9,8},{10,11... | collective-permute-start | bytes 393224 | tf_op jit(solution)/shard_map/ppermute | solution.py:22
  58.1 6.7 %collective-permute-start.8 = (bf16[1024,128]{1,0:T(8,128)(2,1)S(1)}, bf16[1024,128]{1,0:T(8,128)(2,1)S(1)}, u32[]{:S(2)}, u32[]{:S(2)}) collective-permute-start(bf16[1024,128]{1,0:T(8,128)(2,1)S(1)} %pad_maximum_fusion), channel_id=1, source_target_pairs={{0,24},{8,0},{16,8},{24,16},{1,25},{9,1},{17,9},{25,17},{2,26},{10... | collective-permute-start | bytes 786440 | tf_op jit(solution)/shard_map/ppermute | solution.py:22
  59.6 7.3 %collective-permute-start.9 = (bf16[1024,128]{1,0:T(8,128)(2,1)S(1)}, bf16[1024,128]{1,0:T(8,128)(2,1)S(1)}, u32[]{:S(2)}, u32[]{:S(2)}) collective-permute-start(bf16[1024,128]{1,0:T(8,128)(2,1)S(1)} %pad_maximum_fusion), channel_id=1, source_target_pairs={{0,8},{8,16},{16,24},{24,0},{1,9},{9,17},{17,25},{25,1},{2,10},{10... | collective-permute-start | bytes 786440 | tf_op jit(solution)/shard_map/ppermute | solution.py:22
  67.6 6.2 %collective-permute-start.10 = (bf16[512,128]{1,0:T(8,128)(2,1)S(1)}, bf16[512,128]{1,0:T(8,128)(2,1)S(1)}, u32[]{:S(2)}, u32[]{:S(2)}) collective-permute-start(bf16[512,128]{1,0:T(8,128)(2,1)S(1)} %slice.105), channel_id=1, source_target_pairs={{0,24},{8,0},{16,8},{24,16},{1,25},{9,1},{17,9},{25,17},{2,26},{10... | collective-permute-start | bytes 393224 | tf_op jit(solution)/shard_map/ppermute | solution.py:22
  68.7 5.1 %collective-permute-start.11 = (bf16[512,128]{1,0:T(8,128)(2,1)S(1)}, bf16[512,128]{1,0:T(8,128)(2,1)S(1)}, u32[]{:S(2)}, u32[]{:S(2)}) collective-permute-start(bf16[512,128]{1,0:T(8,128)(2,1)S(1)} %slice.106), channel_id=1, source_target_pairs={{0,8},{8,16},{16,24},{24,0},{1,9},{9,17},{17,25},{25,1},{2,10},{10... | collective-permute-start | bytes 393224 | tf_op jit(solution)/shard_map/ppermute | solution.py:22
  75.4 5.1 %collective-permute-start.12 = (bf16[128,1024]{1,0:T(8,128)(2,1)S(1)}, bf16[128,1024]{1,0:T(8,128)(2,1)S(1)}, u32[]{:S(2)}, u32[]{:S(2)}) collective-permute-start(bf16[128,1024]{1,0:T(8,128)(2,1)S(1)} %slice.194), channel_id=1, source_target_pairs={{0,32},{32,0},{1,33},{33,1},{2,34},{34,2},{3,35},{35,3},{4,36},{36... | collective-permute-start | bytes 786440 | tf_op jit(solution)/shard_map/ppermute | solution.py:22
  80.6 9.1 %collective-permute-start.14 = (bf16[128,1024]{1,0:T(8,128)(2,1)S(1)}, bf16[128,1024]{1,0:T(8,128)(2,1)S(1)}, u32[]{:S(2)}, u32[]{:S(2)}) collective-permute-start(bf16[128,1024]{1,0:T(8,128)(2,1)S(1)} %fusion.21), channel_id=1, source_target_pairs={{0,128},{64,192},{128,0},{192,64},{1,129},{65,193},{129,1},{193,65... | collective-permute-start | bytes 786440 | tf_op jit(solution)/shard_map/ppermute | solution.py:22
  81.8 7.9 %collective-permute-start.13 = (bf16[128,1024]{1,0:T(8,128)(2,1)S(1)}, bf16[128,1024]{1,0:T(8,128)(2,1)S(1)}, u32[]{:S(2)}, u32[]{:S(2)}) collective-permute-start(bf16[128,1024]{1,0:T(8,128)(2,1)S(1)} %get-tuple-element.47), channel_id=1, source_target_pairs={{0,32},{32,0},{1,33},{33,1},{2,34},{34,2},{3,35},{35,3},{4,36},{36... | collective-permute-start | bytes 786440 | tf_op jit(solution)/shard_map/ppermute | solution.py:22
  82.5 1.5 %collective-permute-start.17 = (bf16[128,1024]{1,0:T(8,128)(2,1)S(1)}, bf16[128,1024]{1,0:T(8,128)(2,1)S(1)}, u32[]{:S(2)}, u32[]{:S(2)}) collective-permute-start(bf16[128,1024]{1,0:T(8,128)(2,1)S(1)} %get-tuple-element.48), channel_id=1, source_target_pairs={{0,32},{32,0},{1,33},{33,1},{2,34},{34,2},{3,35},{35,3},{4,36},{36... | collective-permute-start | bytes 786440 | tf_op jit(solution)/shard_map/ppermute | solution.py:22
  82.6 1.8 %collective-permute-start.15 = (bf16[128,1024]{1,0:T(8,128)(2,1)S(1)}, bf16[128,1024]{1,0:T(8,128)(2,1)S(1)}, u32[]{:S(2)}, u32[]{:S(2)}) collective-permute-start(bf16[128,1024]{1,0:T(8,128)(2,1)S(1)} %get-tuple-element.49), channel_id=1, source_target_pairs={{0,32},{32,0},{1,33},{33,1},{2,34},{34,2},{3,35},{35,3},{4,36},{36... | collective-permute-start | bytes 786440 | tf_op jit(solution)/shard_map/ppermute | solution.py:22
  84.6 11.4 %collective-permute-start.16 = (bf16[128,1024]{1,0:T(8,128)(2,1)S(1)}, bf16[128,1024]{1,0:T(8,128)(2,1)S(1)}, u32[]{:S(2)}, u32[]{:S(2)}) collective-permute-start(bf16[128,1024]{1,0:T(8,128)(2,1)S(1)} %get-tuple-element.45), channel_id=1, source_target_pairs={{0,64},{64,128},{128,192},{192,0},{1,65},{65,129},{129,193},{193,1... | collective-permute-start | bytes 786440 | tf_op jit(solution)/shard_map/ppermute | solution.py:22
  84.7 11.4 %collective-permute-start.18 = (bf16[128,1024]{1,0:T(8,128)(2,1)S(1)}, bf16[128,1024]{1,0:T(8,128)(2,1)S(1)}, u32[]{:S(2)}, u32[]{:S(2)}) collective-permute-start(bf16[128,1024]{1,0:T(8,128)(2,1)S(1)} %get-tuple-element.46), channel_id=1, source_target_pairs={{0,192},{64,0},{128,64},{192,128},{1,193},{65,1},{129,65},{193,129... | collective-permute-start | bytes 786440 | tf_op jit(solution)/shard_map/ppermute | solution.py:22

commit v3 on v2

--- a/solution.py
+++ b/solution.py
@@ -74,9 +74,10 @@
     live = lax.iota(jnp.int32, rows.shape[0]) < count[0]
     x, z = rows // NZ, rows % NZ
     high, deep = z // NL, z % NL
-    sent_at = (x * NL + deep) * NH + high
     far = (x - lax.axis_index("x") + NX) % NX
-    z_at = (deep + lax.axis_index("zl")) % NL * NH + high
+    beside = (deep + lax.axis_index("zl")) % NL
+    sent_at = (far * NL + beside) * NH + high
+    z_at = beside * NH + high
     held_at = jnp.where(far < 2, far, 5 - far) * NZ + z_at
     late = NC + (1 - other) * (NY - 1) + jnp.where(off == 0, 2, off // 2)
     order = jnp.where(off == 2, 1 - other, late)
@@ -96,8 +97,13 @@
     column = jnp.concatenate([p[:BLOCK] for p in near] + [p[BLOCK:] for p in near], 0)
 
     terms = jnp.dot(dense, column, preferred_element_type=F32).astype(BF)
-    swapped = lax.all_to_all(terms, ("x", "zl"), 0, 0, tiled=True)
-    sent = swapped.reshape(NX * NL, NH * BLOCK, -1).astype(F32).sum(0).astype(BF)
+    part = NH * BLOCK
+    total = terms[:part].astype(F32)
+    for a, b in ((2, 1), (2, 0), (1, 1), (3, 1), (1, 0), (3, 0), (0, 1)):
+        start = (a * NL + b) * part
+        ring = [((i + a) % NX) * NL + (j + b) % NL for i in range(NX) for j in range(NL)]
+        total += lax.ppermute(terms[start : start + part], ("x", "zl"), list(enumerate(ring))).astype(F32)
+    sent = total.astype(BF)
     got = {i: shift(sent, "zh", NH, i) for i in (1, 3, 2)}
     code, got[2] = lax.optimization_barrier((code, got[2]))
     dense_t = place(True, code, tile_values)

time: 97.5 us -> 94.9 us (0.973)
  blocking collectives: 19.2 us -> 0 us
  starting transfers between devices: 28.7 us -> 39.7 us
  waiting for transfers between devices: 23.8 us -> 29.2 us
    all_to_all x1 -> x0, blocking collectives: 19.2 us -> none  [body(): swapped = lax.all_to_all(terms, ('x', 'zl'), 0, 0, tiled=True)]
    ppermute x0 -> x7, starting transfers between devices: none -> 10.3 us  [body(): lax.ppermute(terms[start:start + part], ('x', 'zl'), list(enumerate(ring)))]
    ppermute x0 -> x7, waiting for transfers between devices: none -> 6.89 us  [body(): lax.ppermute(terms[start:start + part], ('x', 'zl'), list(enumerate(ring)))]
    ppermute x19, waiting for transfers between devices: 23.8 us -> 22.3 us  [shift(): lax.ppermute(value, axis, [(i, (i + step) % size) for i in range(size)])]
  transfers between devices with their start and end apart: 19 -> 26, of which waited for: 10 -> 14; matrix products, arithmetic and copies ran while one was open for 12% -> 13% of each run, Pallas kernels for 7% -> 7%
where the time goes in v3:
time: 94.9 us; the launch traced here: 94.8 us
  starting transfers between devices  39.7 us (42%)
  waiting for transfers between devices  29.2 us (31%)
  matrix products  16.3 us (17%)
  Pallas kernels  6.36 us (7%)
  other arithmetic  1.17 us (1%)
  local copies, waits for them, and re-layouts  1.03 us (1%)
    ppermute x19, starting transfers between devices, shift(): lax.ppermute(value, axis, [(i, (i + step) % size) for i in range(size)])  29.5 us
    ppermute x19, waiting for transfers between devices, shift(): lax.ppermute(value, axis, [(i, (i + step) % size) for i in range(size)])  22.3 us
    ppermute x7, starting transfers between devices, body(): lax.ppermute(terms[start:start + part], ('x', 'zl'), list(enumerate(ring)))  10.3 us
    dot_general x6, matrix products, second(): return jnp.dot(dense_t[rows, cols], states, preferred_element_type=F32)  9.79 us
    ppermute x7, waiting for transfers between devices, body(): lax.ppermute(terms[start:start + part], ('x', 'zl'), list(enumerate(ring)))  6.89 us
    pallas_call x2, Pallas kernels, place(): pl.pallas_call(functools.partial(place_kernel, transposed), in_specs=[pl....  6.36 us
    dot_general x4, matrix products, hidden(): states = jax.nn.relu(jnp.dot(panel, weight_in, preferred_element_type=F32))  2.78 us
    dot_general x1, matrix products, body(): terms = jnp.dot(dense, column, preferred_element_type=F32).astype(BF)  2.53 us
  transfers between devices with their start and end apart: 26, of which 14 were waited for; matrix products, arithmetic and copies ran while one was open for 13% of the time, Pallas kernels for 7%

profile of v3, /device:TPU:1, one launch (start us, length us, event | category | flops | bytes accessed | tf_op | source)
XLA Modules:
  0.0 94.8 jit_solution(2982060645914003232)
XLA Ops:
  0.0 3.2 %collective-permute-start = (bf16[128,128]{1,0:T(8,128)(2,1)}, bf16[128,128]{1,0:T(8,128)(2,1)S(1)}, u32[]{:S(2)}, u32[]{:S(2)}) collective-permute-start(bf16[128,128]{1,0:T(8,128)(2,1)} %param.7), channel_id=1, source_target_pairs={{0,32},{32,0},{1,33},{33,1},{2,34},{34,2},{3,35},{35,3},{4,36},{36... | collective-permute-start | bytes 98312 | tf_op jit(solution)/shard_map/ppermute | solution.py:22
  3.2 0.8 constant_dynamic-update-slice_fusion.3
  4.7 1.3 %collective-permute-start.1 = (bf16[256,128]{1,0:T(8,128)(2,1)S(1)}, bf16[256,128]{1,0:T(8,128)(2,1)S(1)}, u32[]{:S(2)}, u32[]{:S(2)}) collective-permute-start(bf16[256,128]{1,0:T(8,128)(2,1)S(1)} %constant_dynamic-update-slice_fusion), channel_id=1, source_target_pairs={{0,128},{64,192},{128,0},{192,64},{1,129},{65,193},{129,1},{193,65... | collective-permute-start | bytes 196616 | tf_op jit(solution)/shard_map/ppermute | solution.py:22
  6.0 0.7 fusion.26.code
  6.7 0.5 collective-permute-start.3
  7.1 2.3 %collective-permute-start.2 = (bf16[256,128]{1,0:T(8,128)(2,1)S(1)}, bf16[256,128]{1,0:T(8,128)(2,1)S(1)}, u32[]{:S(2)}, u32[]{:S(2)}) collective-permute-start(bf16[256,128]{1,0:T(8,128)(2,1)S(1)} %constant_dynamic-update-slice_fusion), channel_id=1, source_target_pairs={{0,192},{64,0},{128,64},{192,128},{1,193},{65,1},{129,65},{193,129... | collective-permute-start | bytes 196616 | tf_op jit(solution)/shard_map/ppermute | solution.py:22
  9.4 0.4 collective-permute-done.1
  9.8 3.0 %place.1 = bf16[4096,1024]{1,0:T(8,128)(2,1)S(1)} custom-call(s32[128]{0:T(128)S(1)} %fusion.26.code, bf16[128,128,128]{2,1,0:T(8,128)(2,1)} %tiles.3), custom_call_target="tpu_custom_call" | custom-call | flops 10000000000 | bytes 16777216 | tf_op jit(solution)/shard_map/place/pallas_call | solution.py:53
  12.9 2.5 %convolution_convert_fusion = bf16[4096,128]{1,0:T(8,128)(2,1)S(1)} fusion(bf16[4096,1024]{1,0:T(8,128)(2,1)S(1)} %place.1, bf16[1024,128]{1,0:T(8,128)(2,1)S(1)} %slice_dynamic-update-slice_fusion), kind=kOutput, calls=%fused_computation | convolution fusion | flops 1074266112 | bytes 9699328 | tf_op jit(solution)/shard_map/dot_general | solution.py:99
  15.5 3.8 %collective-permute-start.4 = (bf16[512,128]{1,0:T(8,128)(2,1)S(1)}, bf16[512,128]{1,0:T(8,128)(2,1)S(1)}, u32[]{:S(2)}, u32[]{:S(2)}) collective-permute-start(bf16[512,128]{1,0:T(8,128)(2,1)S(1)} %get-tuple-element.47), channel_id=1, source_target_pairs={{0,17},{1,16},{8,25},{9,24},{16,1},{17,0},{24,9},{25,8},{2,19},{3,... | collective-permute-start | bytes 393224 | tf_op jit(solution)/shard_map/ppermute | solution.py:105
  19.3 0.9 collective-permute-start.9
  20.2 0.6 collective-permute-start.8
  20.8 3.3 %collective-permute-start.7 = (bf16[512,128]{1,0:T(8,128)(2,1)S(1)}, bf16[512,128]{1,0:T(8,128)(2,1)S(1)}, u32[]{:S(2)}, u32[]{:S(2)}) collective-permute-start(bf16[512,128]{1,0:T(8,128)(2,1)S(1)} %get-tuple-element.51), channel_id=1, source_target_pairs={{0,25},{1,24},{8,1},{9,0},{16,9},{17,8},{24,17},{25,16},{2,27},{3,... | collective-permute-start | bytes 393224 | tf_op jit(solution)/shard_map/ppermute | solution.py:105
  24.1 0.7 collective-permute-done.10
  24.8 1.7 %collective-permute-start.5 = (bf16[512,128]{1,0:T(8,128)(2,1)S(1)}, bf16[512,128]{1,0:T(8,128)(2,1)S(1)}, u32[]{:S(2)}, u32[]{:S(2)}) collective-permute-start(bf16[512,128]{1,0:T(8,128)(2,1)S(1)} %get-tuple-element.53), channel_id=1, source_target_pairs={{0,16},{1,17},{8,24},{9,25},{16,0},{17,1},{24,8},{25,9},{2,18},{3,... | collective-permute-start | bytes 393224 | tf_op jit(solution)/shard_map/ppermute | solution.py:105
  26.5 1.2 %collective-permute-done.7 = bf16[512,128]{1,0:T(8,128)(2,1)S(1)} collective-permute-done((bf16[512,128]{1,0:T(8,128)(2,1)S(1)}, bf16[512,128]{1,0:T(8,128)(2,1)S(1)}, u32[]{:S(2)}, u32[]{:S(2)}) %collective-permute-start.7) | collective-permute-done | bytes 131104 | tf_op jit(solution)/shard_map/ppermute | solution.py:105
  27.7 3.4 %collective-permute-done.6 = bf16[512,128]{1,0:T(8,128)(2,1)S(1)} collective-permute-done((bf16[512,128]{1,0:T(8,128)(2,1)S(1)}, bf16[512,128]{1,0:T(8,128)(2,1)S(1)}, u32[]{:S(2)}, u32[]{:S(2)}) %collective-permute-start.6) | collective-permute-done | bytes 131104 | tf_op jit(solution)/shard_map/ppermute | solution.py:105
  31.0 1.6 %collective-permute-done.5 = bf16[512,128]{1,0:T(8,128)(2,1)S(1)} collective-permute-done((bf16[512,128]{1,0:T(8,128)(2,1)S(1)}, bf16[512,128]{1,0:T(8,128)(2,1)S(1)}, u32[]{:S(2)}, u32[]{:S(2)}) %collective-permute-start.5) | collective-permute-done | bytes 131104 | tf_op jit(solution)/shard_map/ppermute | solution.py:105
  32.9 5.4 %collective-permute-start.11 = (bf16[512,128]{1,0:T(8,128)(2,1)S(1)}, bf16[512,128]{1,0:T(8,128)(2,1)S(1)}, u32[]{:S(2)}, u32[]{:S(2)}) collective-permute-start(bf16[512,128]{1,0:T(8,128)(2,1)S(1)} %add_convert_fusion.1), channel_id=1, source_target_pairs={{0,4},{2,6},{4,0},{6,2},{1,5},{3,7},{5,1},{7,3},{8,12},{10,14},{12... | collective-permute-start | bytes 393224 | tf_op jit(solution)/shard_map/ppermute | solution.py:22
  38.2 2.4 %collective-permute-start.12 = (bf16[512,128]{1,0:T(8,128)(2,1)S(1)}, bf16[512,128]{1,0:T(8,128)(2,1)S(1)}, u32[]{:S(2)}, u32[]{:S(2)}) collective-permute-start(bf16[512,128]{1,0:T(8,128)(2,1)S(1)} %add_convert_fusion.1), channel_id=1, source_target_pairs={{0,2},{2,4},{4,6},{6,0},{1,3},{3,5},{5,7},{7,1},{8,10},{10,12},{12... | collective-permute-start | bytes 393224 | tf_op jit(solution)/shard_map/ppermute | solution.py:22
  40.9 3.4 %place_t.1 = bf16[1024,4096]{1,0:T(8,128)(2,1)S(1)} custom-call(s32[128]{0:T(128)S(1)} %fusion.26.code, bf16[128,128,128]{2,1,0:T(8,128)(2,1)} %tiles.3), custom_call_target="tpu_custom_call" | custom-call | flops 10000000000 | bytes 16777216 | tf_op jit(solution)/shard_map/place_t/pallas_call | solution.py:53
  44.4 6.2 %collective-permute-done.13 = bf16[512,128]{1,0:T(8,128)(2,1)S(1)} collective-permute-done((bf16[512,128]{1,0:T(8,128)(2,1)S(1)}, bf16[512,128]{1,0:T(8,128)(2,1)S(1)}, u32[]{:S(2)}, u32[]{:S(2)}) %collective-permute-start.13) | collective-permute-done | bytes 131104 | tf_op jit(solution)/shard_map/ppermute | solution.py:22
  50.6 1.0 %collective-permute-start.14 = (bf16[512,128]{1,0:T(8,128)(2,1)S(1)}, bf16[512,128]{1,0:T(8,128)(2,1)S(1)}, u32[]{:S(2)}, u32[]{:S(2)}) collective-permute-start(bf16[512,128]{1,0:T(8,128)(2,1)S(1)} %add_convert_fusion), channel_id=1, source_target_pairs={{0,1},{1,0},{2,3},{3,2},{4,5},{5,4},{6,7},{7,6},{8,9},{9,8},{10,11... | collective-permute-start | bytes 393224 | tf_op jit(solution)/shard_map/ppermute | solution.py:22
  51.6 2.9 %collective-permute-done.14 = bf16[512,128]{1,0:T(8,128)(2,1)S(1)} collective-permute-done((bf16[512,128]{1,0:T(8,128)(2,1)S(1)}, bf16[512,128]{1,0:T(8,128)(2,1)S(1)}, u32[]{:S(2)}, u32[]{:S(2)}) %collective-permute-start.14) | collective-permute-done | bytes 131104 | tf_op jit(solution)/shard_map/ppermute | solution.py:22
  54.6 2.7 %collective-permute-start.15 = (bf16[1024,128]{1,0:T(8,128)(2,1)S(1)}, bf16[1024,128]{1,0:T(8,128)(2,1)S(1)}, u32[]{:S(2)}, u32[]{:S(2)}) collective-permute-start(bf16[1024,128]{1,0:T(8,128)(2,1)S(1)} %pad_maximum_fusion), channel_id=1, source_target_pairs={{0,24},{8,0},{16,8},{24,16},{1,25},{9,1},{17,9},{25,17},{2,26},{10... | collective-permute-start | bytes 786440 | tf_op jit(solution)/shard_map/ppermute | solution.py:22
  57.3 0.7 maximum_convert_fusion.3
  58.0 2.3 %fusion.4 = f32[1024,1024]{1,0:T(8,128)S(1)} fusion(bf16[1024,1024]{1,0:T(8,128)(2,1)S(1)} %maximum_convert_fusion.3, bf16[1024,4096]{1,0:T(8,128)(2,1)S(1)} %place_t.1), kind=kOutput, calls=%fused_computation.9 | convolution fusion | flops 2147483648 | bytes 8388608 | tf_op jit(solution)/shard_map/dot_general | solution.py:124
  60.3 0.9 collective-permute-done.15
  61.2 0.7 maximum_convert_fusion.2
  61.9 2.4 %collective-permute-done.16 = bf16[1024,128]{1,0:T(8,128)(2,1)S(1)} collective-permute-done((bf16[1024,128]{1,0:T(8,128)(2,1)S(1)}, bf16[1024,128]{1,0:T(8,128)(2,1)S(1)}, u32[]{:S(2)}, u32[]{:S(2)}) %collective-permute-start.16) | collective-permute-done | bytes 262176 | tf_op jit(solution)/shard_map/ppermute | solution.py:22
  64.4 0.7 maximum_convert_fusion.1
  65.1 1.1 %collective-permute-start.17 = (bf16[512,128]{1,0:T(8,128)(2,1)S(1)}, bf16[512,128]{1,0:T(8,128)(2,1)S(1)}, u32[]{:S(2)}, u32[]{:S(2)}) collective-permute-start(bf16[512,128]{1,0:T(8,128)(2,1)S(1)} %slice.137), channel_id=1, source_target_pairs={{0,24},{8,0},{16,8},{24,16},{1,25},{9,1},{17,9},{25,17},{2,26},{10... | collective-permute-start | bytes 393224 | tf_op jit(solution)/shard_map/ppermute | solution.py:22
  66.1 0.5 collective-permute-start.18
  66.6 2.3 %fusion.2 = f32[1024,1024]{1,0:T(8,128)S(1)} fusion(bf16[1024,1024]{1,0:T(8,128)(2,1)S(1)} %maximum_convert_fusion.2, bf16[1024,4096]{1,0:T(8,128)(2,1)S(1)} %place_t.1), kind=kOutput, calls=%fused_computation.7 | convolution fusion | flops 2147483648 | bytes 8388608 | tf_op jit(solution)/shard_map/dot_general | solution.py:124
  68.9 2.3 %fusion = f32[1024,1024]{1,0:T(8,128)S(1)} fusion(bf16[1024,1024]{1,0:T(8,128)(2,1)S(1)} %maximum_convert_fusion.1, bf16[1024,4096]{1,0:T(8,128)(2,1)S(1)} %place_t.1), kind=kOutput, calls=%fused_computation.5 | convolution fusion | flops 2147483648 | bytes 8388608 | tf_op jit(solution)/shard_map/dot_general | solution.py:124
  71.3 0.7 maximum_convert_fusion
  72.0 0.8 convolution_add_fusion
  72.8 4.0 %collective-permute-start.19 = (bf16[128,1024]{1,0:T(8,128)(2,1)S(1)}, bf16[128,1024]{1,0:T(8,128)(2,1)S(1)}, u32[]{:S(2)}, u32[]{:S(2)}) collective-permute-start(bf16[128,1024]{1,0:T(8,128)(2,1)S(1)} %slice.235), channel_id=1, source_target_pairs={{0,32},{32,0},{1,33},{33,1},{2,34},{34,2},{3,35},{35,3},{4,36},{36... | collective-permute-start | bytes 786440 | tf_op jit(solution)/shard_map/ppermute | solution.py:22
  76.8 1.0 %fusion.8 = bf16[384,1024]{1,0:T(8,128)(2,1)S(1)} fusion(f32[1024,1024]{1,0:T(8,128)S(1)} %fusion.2, f32[1024,1024]{1,0:T(8,128)S(1)} %fusion, f32[1024,1024]{1,0:T(8,128)S(1)} %fusion.4, bf16[1024,1024]{1,0:T(8,128)(2,1)S(1)} %maximum_convert_fusion, bf16[1024,4096]{1,0:T(8,128)(2,1)S(1)} %place_t.1), kind=kOutput, calls=%fused_computation.14 | convolution fusion | flops 806879232 | bytes 8388608 | tf_op jit(solution)/shard_map/dot_general | solution.py:124
  78.1 1.2 %collective-permute-start.21 = (bf16[128,1024]{1,0:T(8,128)(2,1)S(1)}, bf16[128,1024]{1,0:T(8,128)(2,1)S(1)}, u32[]{:S(2)}, u32[]{:S(2)}) collective-permute-start(bf16[128,1024]{1,0:T(8,128)(2,1)S(1)} %fusion.21), channel_id=1, source_target_pairs={{0,128},{64,192},{128,0},{192,64},{1,129},{65,193},{129,1},{193,65... | collective-permute-start | bytes 786440 | tf_op jit(solution)/shard_map/ppermute | solution.py:22
  79.3 0.7 collective-permute-start.20
  80.2 0.4 collective-permute-start.22
  80.6 1.0 %fusion.10 = f32[384,1024]{1,0:T(8,128)S(1)} fusion(f32[1024,1024]{1,0:T(8,128)S(1)} %fusion.2, f32[1024,1024]{1,0:T(8,128)S(1)} %fusion, f32[1024,1024]{1,0:T(8,128)S(1)} %fusion.4, bf16[1024,1024]{1,0:T(8,128)(2,1)S(1)} %maximum_convert_fusion, bf16[1024,4096]{1,0:T(8,128)(2,1)S(1)} %place_t.1), kind=kOutput, calls=%fused_computation.17 | convolution fusion | flops 806486016 | bytes 9175040 | tf_op jit(solution)/shard_map/dot_general | solution.py:124
  82.1 0.7 collective-permute-start.23
  82.8 2.1 %collective-permute-start.25 = (bf16[128,1024]{1,0:T(8,128)(2,1)S(1)}, bf16[128,1024]{1,0:T(8,128)(2,1)S(1)}, u32[]{:S(2)}, u32[]{:S(2)}) collective-permute-start(bf16[128,1024]{1,0:T(8,128)(2,1)S(1)} %get-tuple-element.46), channel_id=1, source_target_pairs={{0,192},{64,0},{128,64},{192,128},{1,193},{65,1},{129,65},{193,129... | collective-permute-start | bytes 786440 | tf_op jit(solution)/shard_map/ppermute | solution.py:22
  84.9 2.3 %collective-permute-done.21 = bf16[128,1024]{1,0:T(8,128)(2,1)S(1)} collective-permute-done((bf16[128,1024]{1,0:T(8,128)(2,1)S(1)}, bf16[128,1024]{1,0:T(8,128)(2,1)S(1)}, u32[]{:S(2)}, u32[]{:S(2)}) %collective-permute-start.21) | collective-permute-done | bytes 262176 | tf_op jit(solution)/shard_map/ppermute | solution.py:22
  87.2 6.3 %collective-permute-done.23 = bf16[128,1024]{1,0:T(8,128)(2,1)S(1)} collective-permute-done((bf16[128,1024]{1,0:T(8,128)(2,1)S(1)}, bf16[128,1024]{1,0:T(8,128)(2,1)S(1)}, u32[]{:S(2)}, u32[]{:S(2)}) %collective-permute-start.23) | collective-permute-done | bytes 262176 | tf_op jit(solution)/shard_map/ppermute | solution.py:22
  93.5 1.2 %fusion.11 = bf16[128,1024]{1,0:T(8,128)(2,1)} fusion(bf16[1024,1024]{1,0:T(8,128)(2,1)S(1)} %copy-done, f32[384,1024]{1,0:T(8,128)S(1)} %fusion.10, bf16[128,1024]{1,0:T(8,128)(2,1)S(1)} %collective-permute-done.25, bf16[128,1024]{1,0:T(8,128)(2,1)S(1)} %collective-permute-done.23, bf16[128,1024]{1,0:T(8,128)(2,1)S(1)} %collective-permute-done.21, ...), kind=kOutput, calls=%fused_computation.20 | convolution fusion | flops 269877248 | bytes 3932160 | tf_op jit(solution)/shard_map/dot_general | solution.py:157
  (43 shorter events, 1.8 us)
Async XLA Ops:
  0.0 93.5 %copy-start = (bf16[1024,1024]{1,0:T(8,128)(2,1)S(1)}, bf16[1024,1024]{1,0:T(8,128)(2,1)}, u32[]{:S(2)}) copy-start(bf16[1024,1024]{1,0:T(8,128)(2,1)} %param.13) | copy-start | bytes 6291460
  0.0 4.7 %collective-permute-start = (bf16[128,128]{1,0:T(8,128)(2,1)}, bf16[128,128]{1,0:T(8,128)(2,1)S(1)}, u32[]{:S(2)}, u32[]{:S(2)}) collective-permute-start(bf16[128,128]{1,0:T(8,128)(2,1)} %param.7), channel_id=1, source_target_pairs={{0,32},{32,0},{1,33},{33,1},{2,34},{34,2},{3,35},{35,3},{4,36},{36... | collective-permute-start | bytes 98312 | tf_op jit(solution)/shard_map/ppermute | solution.py:22
  4.7 5.1 %collective-permute-start.1 = (bf16[256,128]{1,0:T(8,128)(2,1)S(1)}, bf16[256,128]{1,0:T(8,128)(2,1)S(1)}, u32[]{:S(2)}, u32[]{:S(2)}) collective-permute-start(bf16[256,128]{1,0:T(8,128)(2,1)S(1)} %constant_dynamic-update-slice_fusion), channel_id=1, source_target_pairs={{0,128},{64,192},{128,0},{192,64},{1,129},{65,193},{129,1},{193,65... | collective-permute-start | bytes 196616 | tf_op jit(solution)/shard_map/ppermute | solution.py:22
  6.7 6.1 %collective-permute-start.3 = (bf16[256,128]{1,0:T(8,128)(2,1)S(1)}, bf16[256,128]{1,0:T(8,128)(2,1)S(1)}, u32[]{:S(2)}, u32[]{:S(2)}) collective-permute-start(bf16[256,128]{1,0:T(8,128)(2,1)S(1)} %constant_dynamic-update-slice_fusion), channel_id=1, source_target_pairs={{0,64},{64,128},{128,192},{192,0},{1,65},{65,129},{129,193},{193,1... | collective-permute-start | bytes 196616 | tf_op jit(solution)/shard_map/ppermute | solution.py:22
  7.1 5.7 %collective-permute-start.2 = (bf16[256,128]{1,0:T(8,128)(2,1)S(1)}, bf16[256,128]{1,0:T(8,128)(2,1)S(1)}, u32[]{:S(2)}, u32[]{:S(2)}) collective-permute-start(bf16[256,128]{1,0:T(8,128)(2,1)S(1)} %constant_dynamic-update-slice_fusion), channel_id=1, source_target_pairs={{0,192},{64,0},{128,64},{192,128},{1,193},{65,1},{129,65},{193,129... | collective-permute-start | bytes 196616 | tf_op jit(solution)/shard_map/ppermute | solution.py:22
  15.5 8.5 %collective-permute-start.4 = (bf16[512,128]{1,0:T(8,128)(2,1)S(1)}, bf16[512,128]{1,0:T(8,128)(2,1)S(1)}, u32[]{:S(2)}, u32[]{:S(2)}) collective-permute-start(bf16[512,128]{1,0:T(8,128)(2,1)S(1)} %get-tuple-element.47), channel_id=1, source_target_pairs={{0,17},{1,16},{8,25},{9,24},{16,1},{17,0},{24,9},{25,8},{2,19},{3,... | collective-permute-start | bytes 393224 | tf_op jit(solution)/shard_map/ppermute | solution.py:105
  19.3 5.5 %collective-permute-start.10 = (bf16[512,128]{1,0:T(8,128)(2,1)S(1)}, bf16[512,128]{1,0:T(8,128)(2,1)S(1)}, u32[]{:S(2)}, u32[]{:S(2)}) collective-permute-start(bf16[512,128]{1,0:T(8,128)(2,1)S(1)} %get-tuple-element.48), channel_id=1, source_target_pairs={{0,1},{1,0},{8,9},{9,8},{16,17},{17,16},{24,25},{25,24},{2,3},{3,2... | collective-permute-start | bytes 393224 | tf_op jit(solution)/shard_map/ppermute | solution.py:105
  19.3 7.2 %collective-permute-start.9 = (bf16[512,128]{1,0:T(8,128)(2,1)S(1)}, bf16[512,128]{1,0:T(8,128)(2,1)S(1)}, u32[]{:S(2)}, u32[]{:S(2)}) collective-permute-start(bf16[512,128]{1,0:T(8,128)(2,1)S(1)} %get-tuple-element.49), channel_id=1, source_target_pairs={{0,24},{1,25},{8,0},{9,1},{16,8},{17,9},{24,16},{25,17},{2,26},{3,... | collective-permute-start | bytes 393224 | tf_op jit(solution)/shard_map/ppermute | solution.py:105
  20.2 6.3 %collective-permute-start.8 = (bf16[512,128]{1,0:T(8,128)(2,1)S(1)}, bf16[512,128]{1,0:T(8,128)(2,1)S(1)}, u32[]{:S(2)}, u32[]{:S(2)}) collective-permute-start(bf16[512,128]{1,0:T(8,128)(2,1)S(1)} %get-tuple-element.50), channel_id=1, source_target_pairs={{0,8},{1,9},{8,16},{9,17},{16,24},{17,25},{24,0},{25,1},{2,10},{3,... | collective-permute-start | bytes 393224 | tf_op jit(solution)/shard_map/ppermute | solution.py:105
  20.8 6.9 %collective-permute-start.7 = (bf16[512,128]{1,0:T(8,128)(2,1)S(1)}, bf16[512,128]{1,0:T(8,128)(2,1)S(1)}, u32[]{:S(2)}, u32[]{:S(2)}) collective-permute-start(bf16[512,128]{1,0:T(8,128)(2,1)S(1)} %get-tuple-element.51), channel_id=1, source_target_pairs={{0,25},{1,24},{8,1},{9,0},{16,9},{17,8},{24,17},{25,16},{2,27},{3,... | collective-permute-start | bytes 393224 | tf_op jit(solution)/shard_map/ppermute | solution.py:105
  24.0 7.0 %collective-permute-start.6 = (bf16[512,128]{1,0:T(8,128)(2,1)S(1)}, bf16[512,128]{1,0:T(8,128)(2,1)S(1)}, u32[]{:S(2)}, u32[]{:S(2)}) collective-permute-start(bf16[512,128]{1,0:T(8,128)(2,1)S(1)} %get-tuple-element.52), channel_id=1, source_target_pairs={{0,9},{1,8},{8,17},{9,16},{16,25},{17,24},{24,1},{25,0},{2,11},{3,... | collective-permute-start | bytes 393224 | tf_op jit(solution)/shard_map/ppermute | solution.py:105
  24.8 7.9 %collective-permute-start.5 = (bf16[512,128]{1,0:T(8,128)(2,1)S(1)}, bf16[512,128]{1,0:T(8,128)(2,1)S(1)}, u32[]{:S(2)}, u32[]{:S(2)}) collective-permute-start(bf16[512,128]{1,0:T(8,128)(2,1)S(1)} %get-tuple-element.53), channel_id=1, source_target_pairs={{0,16},{1,17},{8,24},{9,25},{16,0},{17,1},{24,8},{25,9},{2,18},{3,... | collective-permute-start | bytes 393224 | tf_op jit(solution)/shard_map/ppermute | solution.py:105
  32.8 24.5 %copy-start.1 = (bf16[128,1024]{1,0:T(8,128)(2,1)S(1)}, bf16[128,1024]{1,0:T(8,128)(2,1)}, u32[]{:S(2)}) copy-start(bf16[128,1024]{1,0:T(8,128)(2,1)} %param.12) | copy-start | bytes 786436
  32.9 8.1 %collective-permute-start.11 = (bf16[512,128]{1,0:T(8,128)(2,1)S(1)}, bf16[512,128]{1,0:T(8,128)(2,1)S(1)}, u32[]{:S(2)}, u32[]{:S(2)}) collective-permute-start(bf16[512,128]{1,0:T(8,128)(2,1)S(1)} %add_convert_fusion.1), channel_id=1, source_target_pairs={{0,4},{2,6},{4,0},{6,2},{1,5},{3,7},{5,1},{7,3},{8,12},{10,14},{12... | collective-permute-start | bytes 393224 | tf_op jit(solution)/shard_map/ppermute | solution.py:22
  38.2 12.3 %collective-permute-start.13 = (bf16[512,128]{1,0:T(8,128)(2,1)S(1)}, bf16[512,128]{1,0:T(8,128)(2,1)S(1)}, u32[]{:S(2)}, u32[]{:S(2)}) collective-permute-start(bf16[512,128]{1,0:T(8,128)(2,1)S(1)} %add_convert_fusion.1), channel_id=1, source_target_pairs={{0,6},{2,0},{4,2},{6,4},{1,7},{3,1},{5,3},{7,5},{8,14},{10,8},{12,... | collective-permute-start | bytes 393224 | tf_op jit(solution)/shard_map/ppermute | solution.py:22
  38.2 12.3 %collective-permute-start.12 = (bf16[512,128]{1,0:T(8,128)(2,1)S(1)}, bf16[512,128]{1,0:T(8,128)(2,1)S(1)}, u32[]{:S(2)}, u32[]{:S(2)}) collective-permute-start(bf16[512,128]{1,0:T(8,128)(2,1)S(1)} %add_convert_fusion.1), channel_id=1, source_target_pairs={{0,2},{2,4},{4,6},{6,0},{1,3},{3,5},{5,7},{7,1},{8,10},{10,12},{12... | collective-permute-start | bytes 393224 | tf_op jit(solution)/shard_map/ppermute | solution.py:22
  50.6 3.9 %collective-permute-start.14 = (bf16[512,128]{1,0:T(8,128)(2,1)S(1)}, bf16[512,128]{1,0:T(8,128)(2,1)S(1)}, u32[]{:S(2)}, u32[]{:S(2)}) collective-permute-start(bf16[512,128]{1,0:T(8,128)(2,1)S(1)} %add_convert_fusion), channel_id=1, source_target_pairs={{0,1},{1,0},{2,3},{3,2},{4,5},{5,4},{6,7},{7,6},{8,9},{9,8},{10,11... | collective-permute-start | bytes 393224 | tf_op jit(solution)/shard_map/ppermute | solution.py:22
  54.6 6.7 %collective-permute-start.15 = (bf16[1024,128]{1,0:T(8,128)(2,1)S(1)}, bf16[1024,128]{1,0:T(8,128)(2,1)S(1)}, u32[]{:S(2)}, u32[]{:S(2)}) collective-permute-start(bf16[1024,128]{1,0:T(8,128)(2,1)S(1)} %pad_maximum_fusion), channel_id=1, source_target_pairs={{0,24},{8,0},{16,8},{24,16},{1,25},{9,1},{17,9},{25,17},{2,26},{10... | collective-permute-start | bytes 786440 | tf_op jit(solution)/shard_map/ppermute | solution.py:22
  57.3 7.0 %collective-permute-start.16 = (bf16[1024,128]{1,0:T(8,128)(2,1)S(1)}, bf16[1024,128]{1,0:T(8,128)(2,1)S(1)}, u32[]{:S(2)}, u32[]{:S(2)}) collective-permute-start(bf16[1024,128]{1,0:T(8,128)(2,1)S(1)} %pad_maximum_fusion), channel_id=1, source_target_pairs={{0,8},{8,16},{16,24},{24,0},{1,9},{9,17},{17,25},{25,1},{2,10},{10... | collective-permute-start | bytes 786440 | tf_op jit(solution)/shard_map/ppermute | solution.py:22
  65.1 6.2 %collective-permute-start.17 = (bf16[512,128]{1,0:T(8,128)(2,1)S(1)}, bf16[512,128]{1,0:T(8,128)(2,1)S(1)}, u32[]{:S(2)}, u32[]{:S(2)}) collective-permute-start(bf16[512,128]{1,0:T(8,128)(2,1)S(1)} %slice.137), channel_id=1, source_target_pairs={{0,24},{8,0},{16,8},{24,16},{1,25},{9,1},{17,9},{25,17},{2,26},{10... | collective-permute-start | bytes 393224 | tf_op jit(solution)/shard_map/ppermute | solution.py:22
  66.1 5.1 %collective-permute-start.18 = (bf16[512,128]{1,0:T(8,128)(2,1)S(1)}, bf16[512,128]{1,0:T(8,128)(2,1)S(1)}, u32[]{:S(2)}, u32[]{:S(2)}) collective-permute-start(bf16[512,128]{1,0:T(8,128)(2,1)S(1)} %slice.138), channel_id=1, source_target_pairs={{0,8},{8,16},{16,24},{24,0},{1,9},{9,17},{17,25},{25,1},{2,10},{10... | collective-permute-start | bytes 393224 | tf_op jit(solution)/shard_map/ppermute | solution.py:22
  72.8 5.2 %collective-permute-start.19 = (bf16[128,1024]{1,0:T(8,128)(2,1)S(1)}, bf16[128,1024]{1,0:T(8,128)(2,1)S(1)}, u32[]{:S(2)}, u32[]{:S(2)}) collective-permute-start(bf16[128,1024]{1,0:T(8,128)(2,1)S(1)} %slice.235), channel_id=1, source_target_pairs={{0,32},{32,0},{1,33},{33,1},{2,34},{34,2},{3,35},{35,3},{4,36},{36... | collective-permute-start | bytes 786440 | tf_op jit(solution)/shard_map/ppermute | solution.py:22
  78.1 9.1 %collective-permute-start.21 = (bf16[128,1024]{1,0:T(8,128)(2,1)S(1)}, bf16[128,1024]{1,0:T(8,128)(2,1)S(1)}, u32[]{:S(2)}, u32[]{:S(2)}) collective-permute-start(bf16[128,1024]{1,0:T(8,128)(2,1)S(1)} %fusion.21), channel_id=1, source_target_pairs={{0,128},{64,192},{128,0},{192,64},{1,129},{65,193},{129,1},{193,65... | collective-permute-start | bytes 786440 | tf_op jit(solution)/shard_map/ppermute | solution.py:22
  79.3 7.9 %collective-permute-start.20 = (bf16[128,1024]{1,0:T(8,128)(2,1)S(1)}, bf16[128,1024]{1,0:T(8,128)(2,1)S(1)}, u32[]{:S(2)}, u32[]{:S(2)}) collective-permute-start(bf16[128,1024]{1,0:T(8,128)(2,1)S(1)} %get-tuple-element.54), channel_id=1, source_target_pairs={{0,32},{32,0},{1,33},{33,1},{2,34},{34,2},{3,35},{35,3},{4,36},{36... | collective-permute-start | bytes 786440 | tf_op jit(solution)/shard_map/ppermute | solution.py:22
  80.1 1.5 %collective-permute-start.24 = (bf16[128,1024]{1,0:T(8,128)(2,1)S(1)}, bf16[128,1024]{1,0:T(8,128)(2,1)S(1)}, u32[]{:S(2)}, u32[]{:S(2)}) collective-permute-start(bf16[128,1024]{1,0:T(8,128)(2,1)S(1)} %get-tuple-element.55), channel_id=1, source_target_pairs={{0,32},{32,0},{1,33},{33,1},{2,34},{34,2},{3,35},{35,3},{4,36},{36... | collective-permute-start | bytes 786440 | tf_op jit(solution)/shard_map/ppermute | solution.py:22
  80.2 1.8 %collective-permute-start.22 = (bf16[128,1024]{1,0:T(8,128)(2,1)S(1)}, bf16[128,1024]{1,0:T(8,128)(2,1)S(1)}, u32[]{:S(2)}, u32[]{:S(2)}) collective-permute-start(bf16[128,1024]{1,0:T(8,128)(2,1)S(1)} %get-tuple-element.56), channel_id=1, source_target_pairs={{0,32},{32,0},{1,33},{33,1},{2,34},{34,2},{3,35},{35,3},{4,36},{36... | collective-permute-start | bytes 786440 | tf_op jit(solution)/shard_map/ppermute | solution.py:22
  82.1 11.4 %collective-permute-start.23 = (bf16[128,1024]{1,0:T(8,128)(2,1)S(1)}, bf16[128,1024]{1,0:T(8,128)(2,1)S(1)}, u32[]{:S(2)}, u32[]{:S(2)}) collective-permute-start(bf16[128,1024]{1,0:T(8,128)(2,1)S(1)} %get-tuple-element.45), channel_id=1, source_target_pairs={{0,64},{64,128},{128,192},{192,0},{1,65},{65,129},{129,193},{193,1... | collective-permute-start | bytes 786440 | tf_op jit(solution)/shard_map/ppermute | solution.py:22
  82.8 10.7 %collective-permute-start.25 = (bf16[128,1024]{1,0:T(8,128)(2,1)S(1)}, bf16[128,1024]{1,0:T(8,128)(2,1)S(1)}, u32[]{:S(2)}, u32[]{:S(2)}) collective-permute-start(bf16[128,1024]{1,0:T(8,128)(2,1)S(1)} %get-tuple-element.46), channel_id=1, source_target_pairs={{0,192},{64,0},{128,64},{192,128},{1,193},{65,1},{129,65},{193,129... | collective-permute-start | bytes 786440 | tf_op jit(solution)/shard_map/ppermute | solution.py:22

commit v4 on v3

--- a/solution.py
+++ b/solution.py
@@ -77,8 +77,8 @@
     far = (x - lax.axis_index("x") + NX) % NX
     beside = (deep + lax.axis_index("zl")) % NL
     sent_at = (far * NL + beside) * NH + high
-    z_at = beside * NH + high
-    held_at = jnp.where(far < 2, far, 5 - far) * NZ + z_at
+    half = jnp.where(far % 2 == 0, far * 3 + beside, 2 + far // 2 + beside * 2)
+    held_at = half * NH + high
     late = NC + (1 - other) * (NY - 1) + jnp.where(off == 0, 2, off // 2)
     order = jnp.where(off == 2, 1 - other, late)
     word = (held_at * (NX * NZ) + sent_at) * COLS + order
@@ -110,10 +110,9 @@
     dense_t, got[1], got[3] = lax.optimization_barrier((dense_t, got[1], got[3]))
     own = sent.astype(F32) + got[1].astype(F32) + got[3].astype(F32) + got[2].astype(F32)
     own = own.astype(BF)
-    near = jnp.concatenate([own, shift(own, "zl", NL, 1)], 0)
-
-    def fetch(panel, i):
-        return shift(panel, "x", NX, (NX - i) % NX)
+    def fetch(own, a, b):
+        ring = [((i - a) % NX) * NL + (j - b) % NL for i in range(NX) for j in range(NL)]
+        return lax.ppermute(own, ("x", "zl"), list(enumerate(ring)))
 
     def hidden(panel):
         states = jax.nn.relu(jnp.dot(panel, weight_in, preferred_element_type=F32))
@@ -124,17 +123,17 @@
         return jnp.dot(dense_t[rows, cols], states, preferred_element_type=F32)
 
     every = slice(None)
-    one, three = fetch(near, 1), fetch(near, 3)
-    states, near = lax.optimization_barrier((hidden(near), near))
+    near, pair = [own, fetch(own, 0, 1)], [fetch(own, 1, 0), fetch(own, 3, 0)]
+    states, own = lax.optimization_barrier((hidden(jnp.concatenate(near, 0)), own))
+    beside = [fetch(own, 1, 1), fetch(own, 3, 1)]
     term = second(0, every, states)
-    term, one = lax.optimization_barrier((term, one))
-    term, three = lax.optimization_barrier((term, three))
-    term1 = second(1, every, hidden(one))
-    halves = [fetch(one[: SIDE // 2], 1), fetch(three[SIDE // 2 :], 3)]
-    two = jnp.concatenate(halves, 0)
-    term3 = second(2, every, hidden(three))
-    term3, two = lax.optimization_barrier((term3, two))
-    two = hidden(two)
+    term, pair, own = lax.optimization_barrier((term, pair, own))
+    distant = [fetch(own, 2, 0), fetch(own, 2, 1)]
+    term1 = second(1, every, hidden(jnp.concatenate(pair, 0)))
+    term1, beside = lax.optimization_barrier((term1, beside))
+    term3 = second(2, every, hidden(jnp.concatenate(beside, 0)))
+    term3, distant = lax.optimization_barrier((term3, distant))
+    two = hidden(jnp.concatenate(distant, 0))
 
     def final(start, count, states):
         rows = slice(start * BLOCK, (start + count) * BLOCK)

time: 94.9 us -> 94 us (level)
  waiting for transfers between devices: 29.2 us -> 21.8 us
  starting transfers between devices: 39.7 us -> 46.2 us
    ppermute x0 -> x7, starting transfers between devices: none -> 11 us  [fetch(): return lax.ppermute(own, ('x', 'zl'), list(enumerate(ring)))]
    ppermute x19 -> x14, waiting for transfers between devices: 22.3 us -> 14.7 us  [shift(): lax.ppermute(value, axis, [(i, (i + step) % size) for i in range(size)])]
    ppermute x19 -> x14, starting transfers between devices: 29.5 us -> 24.9 us  [shift(): lax.ppermute(value, axis, [(i, (i + step) % size) for i in range(size)])]
  transfers between devices with their start and end apart: 26 -> 28, of which waited for: 14 -> 12; matrix products, arithmetic and copies ran while one was open for 13% -> 14% of each run, Pallas kernels for 7% -> 7%
where the time goes in v4:
time: 94 us; the launch traced here: 93.9 us
  starting transfers between devices  46.2 us (49%)
  waiting for transfers between devices  21.8 us (23%)
  matrix products  16.3 us (17%)
  Pallas kernels  6.36 us (7%)
  other arithmetic  1.14 us (1%)
  local copies, waits for them, and re-layouts  1.01 us (1%)
    ppermute x14, starting transfers between devices, shift(): lax.ppermute(value, axis, [(i, (i + step) % size) for i in range(size)])  24.9 us
    ppermute x14, waiting for transfers between devices, shift(): lax.ppermute(value, axis, [(i, (i + step) % size) for i in range(size)])  14.7 us
    ppermute x7, starting transfers between devices, fetch(): return lax.ppermute(own, ('x', 'zl'), list(enumerate(ring)))  11 us
    ppermute x7, starting transfers between devices, body(): lax.ppermute(terms[start:start + part], ('x', 'zl'), list(enumerate(ring)))  10.3 us
    dot_general x6, matrix products, second(): return jnp.dot(dense_t[rows, cols], states, preferred_element_type=F32)  9.79 us
    ppermute x7, waiting for transfers between devices, body(): lax.ppermute(terms[start:start + part], ('x', 'zl'), list(enumerate(ring)))  6.87 us
    pallas_call x2, Pallas kernels, place(): pl.pallas_call(functools.partial(place_kernel, transposed), in_specs=[pl....  6.36 us
    dot_general x4, matrix products, hidden(): states = jax.nn.relu(jnp.dot(panel, weight_in, preferred_element_type=F32))  2.78 us
  transfers between devices with their start and end apart: 28, of which 12 were waited for; matrix products, arithmetic and copies ran while one was open for 14% of the time, Pallas kernels for 7%

profile of v4, /device:TPU:1, one launch (start us, length us, event | category | flops | bytes accessed | tf_op | source)
XLA Modules:
  0.0 93.9 jit_solution(9890151188920531232)
XLA Ops:
  0.0 3.2 %collective-permute-start = (bf16[128,128]{1,0:T(8,128)(2,1)}, bf16[128,128]{1,0:T(8,128)(2,1)S(1)}, u32[]{:S(2)}, u32[]{:S(2)}) collective-permute-start(bf16[128,128]{1,0:T(8,128)(2,1)} %param.7), channel_id=1, source_target_pairs={{0,32},{32,0},{1,33},{33,1},{2,34},{34,2},{3,35},{35,3},{4,36},{36... | collective-permute-start | bytes 98312 | tf_op jit(solution)/shard_map/ppermute | solution.py:22
  3.2 0.8 constant_dynamic-update-slice_fusion.3
  4.7 1.3 %collective-permute-start.1 = (bf16[256,128]{1,0:T(8,128)(2,1)S(1)}, bf16[256,128]{1,0:T(8,128)(2,1)S(1)}, u32[]{:S(2)}, u32[]{:S(2)}) collective-permute-start(bf16[256,128]{1,0:T(8,128)(2,1)S(1)} %constant_dynamic-update-slice_fusion), channel_id=1, source_target_pairs={{0,128},{64,192},{128,0},{192,64},{1,129},{65,193},{129,1},{193,65... | collective-permute-start | bytes 196616 | tf_op jit(solution)/shard_map/ppermute | solution.py:22
  6.0 0.7 fusion.41.code
  6.7 0.5 collective-permute-start.3
  7.1 2.3 %collective-permute-start.2 = (bf16[256,128]{1,0:T(8,128)(2,1)S(1)}, bf16[256,128]{1,0:T(8,128)(2,1)S(1)}, u32[]{:S(2)}, u32[]{:S(2)}) collective-permute-start(bf16[256,128]{1,0:T(8,128)(2,1)S(1)} %constant_dynamic-update-slice_fusion), channel_id=1, source_target_pairs={{0,192},{64,0},{128,64},{192,128},{1,193},{65,1},{129,65},{193,129... | collective-permute-start | bytes 196616 | tf_op jit(solution)/shard_map/ppermute | solution.py:22
  9.4 0.4 collective-permute-done.1
  9.8 3.0 %place.1 = bf16[4096,1024]{1,0:T(8,128)(2,1)S(1)} custom-call(s32[128]{0:T(128)S(1)} %fusion.41.code, bf16[128,128,128]{2,1,0:T(8,128)(2,1)} %tiles.3), custom_call_target="tpu_custom_call" | custom-call | flops 10000000000 | bytes 16777216 | tf_op jit(solution)/shard_map/place/pallas_call | solution.py:53
  12.9 2.5 %convolution_convert_fusion = bf16[4096,128]{1,0:T(8,128)(2,1)S(1)} fusion(bf16[4096,1024]{1,0:T(8,128)(2,1)S(1)} %place.1, bf16[1024,128]{1,0:T(8,128)(2,1)S(1)} %slice_dynamic-update-slice_fusion), kind=kOutput, calls=%fused_computation | convolution fusion | flops 1074266112 | bytes 9699328 | tf_op jit(solution)/shard_map/dot_general | solution.py:99
  15.5 3.8 %collective-permute-start.4 = (bf16[512,128]{1,0:T(8,128)(2,1)S(1)}, bf16[512,128]{1,0:T(8,128)(2,1)S(1)}, u32[]{:S(2)}, u32[]{:S(2)}) collective-permute-start(bf16[512,128]{1,0:T(8,128)(2,1)S(1)} %get-tuple-element.57), channel_id=1, source_target_pairs={{0,17},{1,16},{8,25},{9,24},{16,1},{17,0},{24,9},{25,8},{2,19},{3,... | collective-permute-start | bytes 393224 | tf_op jit(solution)/shard_map/ppermute | solution.py:105
  19.3 0.9 collective-permute-start.9
  20.2 0.6 collective-permute-start.8
  20.8 3.2 %collective-permute-start.7 = (bf16[512,128]{1,0:T(8,128)(2,1)S(1)}, bf16[512,128]{1,0:T(8,128)(2,1)S(1)}, u32[]{:S(2)}, u32[]{:S(2)}) collective-permute-start(bf16[512,128]{1,0:T(8,128)(2,1)S(1)} %get-tuple-element.61), channel_id=1, source_target_pairs={{0,25},{1,24},{8,1},{9,0},{16,9},{17,8},{24,17},{25,16},{2,27},{3,... | collective-permute-start | bytes 393224 | tf_op jit(solution)/shard_map/ppermute | solution.py:105
  24.2 0.7 collective-permute-done.10
  24.8 1.7 %collective-permute-start.5 = (bf16[512,128]{1,0:T(8,128)(2,1)S(1)}, bf16[512,128]{1,0:T(8,128)(2,1)S(1)}, u32[]{:S(2)}, u32[]{:S(2)}) collective-permute-start(bf16[512,128]{1,0:T(8,128)(2,1)S(1)} %get-tuple-element.63), channel_id=1, source_target_pairs={{0,16},{1,17},{8,24},{9,25},{16,0},{17,1},{24,8},{25,9},{2,18},{3,... | collective-permute-start | bytes 393224 | tf_op jit(solution)/shard_map/ppermute | solution.py:105
  26.5 1.2 %collective-permute-done.7 = bf16[512,128]{1,0:T(8,128)(2,1)S(1)} collective-permute-done((bf16[512,128]{1,0:T(8,128)(2,1)S(1)}, bf16[512,128]{1,0:T(8,128)(2,1)S(1)}, u32[]{:S(2)}, u32[]{:S(2)}) %collective-permute-start.7) | collective-permute-done | bytes 131104 | tf_op jit(solution)/shard_map/ppermute | solution.py:105
  27.7 3.4 %collective-permute-done.6 = bf16[512,128]{1,0:T(8,128)(2,1)S(1)} collective-permute-done((bf16[512,128]{1,0:T(8,128)(2,1)S(1)}, bf16[512,128]{1,0:T(8,128)(2,1)S(1)}, u32[]{:S(2)}, u32[]{:S(2)}) %collective-permute-start.6) | collective-permute-done | bytes 131104 | tf_op jit(solution)/shard_map/ppermute | solution.py:105
  31.1 1.6 %collective-permute-done.5 = bf16[512,128]{1,0:T(8,128)(2,1)S(1)} collective-permute-done((bf16[512,128]{1,0:T(8,128)(2,1)S(1)}, bf16[512,128]{1,0:T(8,128)(2,1)S(1)}, u32[]{:S(2)}, u32[]{:S(2)}) %collective-permute-start.5) | collective-permute-done | bytes 131104 | tf_op jit(solution)/shard_map/ppermute | solution.py:105
  32.9 5.4 %collective-permute-start.11 = (bf16[512,128]{1,0:T(8,128)(2,1)S(1)}, bf16[512,128]{1,0:T(8,128)(2,1)S(1)}, u32[]{:S(2)}, u32[]{:S(2)}) collective-permute-start(bf16[512,128]{1,0:T(8,128)(2,1)S(1)} %add_convert_fusion.2), channel_id=1, source_target_pairs={{0,4},{2,6},{4,0},{6,2},{1,5},{3,7},{5,1},{7,3},{8,12},{10,14},{12... | collective-permute-start | bytes 393224 | tf_op jit(solution)/shard_map/ppermute | solution.py:22
  38.2 2.4 %collective-permute-start.12 = (bf16[512,128]{1,0:T(8,128)(2,1)S(1)}, bf16[512,128]{1,0:T(8,128)(2,1)S(1)}, u32[]{:S(2)}, u32[]{:S(2)}) collective-permute-start(bf16[512,128]{1,0:T(8,128)(2,1)S(1)} %add_convert_fusion.2), channel_id=1, source_target_pairs={{0,2},{2,4},{4,6},{6,0},{1,3},{3,5},{5,7},{7,1},{8,10},{10,12},{12... | collective-permute-start | bytes 393224 | tf_op jit(solution)/shard_map/ppermute | solution.py:22
  40.9 3.4 %place_t.1 = bf16[1024,4096]{1,0:T(8,128)(2,1)S(1)} custom-call(s32[128]{0:T(128)S(1)} %fusion.41.code, bf16[128,128,128]{2,1,0:T(8,128)(2,1)} %tiles.3), custom_call_target="tpu_custom_call" | custom-call | flops 10000000000 | bytes 16777216 | tf_op jit(solution)/shard_map/place_t/pallas_call | solution.py:53
  44.4 6.2 %collective-permute-done.13 = bf16[512,128]{1,0:T(8,128)(2,1)S(1)} collective-permute-done((bf16[512,128]{1,0:T(8,128)(2,1)S(1)}, bf16[512,128]{1,0:T(8,128)(2,1)S(1)}, u32[]{:S(2)}, u32[]{:S(2)}) %collective-permute-start.13) | collective-permute-done | bytes 131104 | tf_op jit(solution)/shard_map/ppermute | solution.py:22
  50.6 1.0 %collective-permute-start.14 = (bf16[512,128]{1,0:T(8,128)(2,1)S(1)}, bf16[512,128]{1,0:T(8,128)(2,1)S(1)}, u32[]{:S(2)}, u32[]{:S(2)}) collective-permute-start(bf16[512,128]{1,0:T(8,128)(2,1)S(1)} %add_convert_fusion.1), channel_id=1, source_target_pairs={{0,1},{1,0},{8,9},{9,8},{16,17},{17,16},{24,25},{25,24},{2,3},{3,2... | collective-permute-start | bytes 393224 | tf_op jit(solution)/shard_map/ppermute | solution.py:115
  51.6 1.4 %collective-permute-start.16 = (bf16[512,128]{1,0:T(8,128)(2,1)S(1)}, bf16[512,128]{1,0:T(8,128)(2,1)S(1)}, u32[]{:S(2)}, u32[]{:S(2)}) collective-permute-start(bf16[512,128]{1,0:T(8,128)(2,1)S(1)} %add_convert_fusion.1), channel_id=1, source_target_pairs={{0,8},{1,9},{8,16},{9,17},{16,24},{17,25},{24,0},{25,1},{2,10},{3,... | collective-permute-start | bytes 393224 | tf_op jit(solution)/shard_map/ppermute | solution.py:115
  53.1 1.2 %collective-permute-start.15 = (bf16[512,128]{1,0:T(8,128)(2,1)S(1)}, bf16[512,128]{1,0:T(8,128)(2,1)S(1)}, u32[]{:S(2)}, u32[]{:S(2)}) collective-permute-start(bf16[512,128]{1,0:T(8,128)(2,1)S(1)} %add_convert_fusion.1), channel_id=1, source_target_pairs={{0,24},{1,25},{8,0},{9,1},{16,8},{17,9},{24,16},{25,17},{2,26},{3,... | collective-permute-start | bytes 393224 | tf_op jit(solution)/shard_map/ppermute | solution.py:115
  54.5 0.7 maximum_convert_fusion.3
  55.2 2.8 %collective-permute-start.18 = (bf16[512,128]{1,0:T(8,128)(2,1)S(1)}, bf16[512,128]{1,0:T(8,128)(2,1)S(1)}, u32[]{:S(2)}, u32[]{:S(2)}) collective-permute-start(bf16[512,128]{1,0:T(8,128)(2,1)S(1)} %add_convert_fusion.1), channel_id=1, source_target_pairs={{0,9},{1,8},{8,17},{9,16},{16,25},{17,24},{24,1},{25,0},{2,11},{3,... | collective-permute-start | bytes 393224 | tf_op jit(solution)/shard_map/ppermute | solution.py:115
  58.1 0.9 collective-permute-start.17
  59.0 2.3 %fusion.4 = f32[1024,1024]{1,0:T(8,128)S(1)} fusion(bf16[1024,1024]{1,0:T(8,128)(2,1)S(1)} %maximum_convert_fusion.3, bf16[1024,4096]{1,0:T(8,128)(2,1)S(1)} %place_t.1), kind=kOutput, calls=%fused_computation.9 | convolution fusion | flops 2147483648 | bytes 8388608 | tf_op jit(solution)/shard_map/dot_general | solution.py:123
  61.4 1.1 %collective-permute-start.20 = (bf16[512,128]{1,0:T(8,128)(2,1)S(1)}, bf16[512,128]{1,0:T(8,128)(2,1)S(1)}, u32[]{:S(2)}, u32[]{:S(2)}) collective-permute-start(bf16[512,128]{1,0:T(8,128)(2,1)S(1)} %add_convert_fusion.1), channel_id=1, source_target_pairs={{0,17},{1,16},{8,25},{9,24},{16,1},{17,0},{24,9},{25,8},{2,19},{3,... | collective-permute-start | bytes 393224 | tf_op jit(solution)/shard_map/ppermute | solution.py:115
  62.5 2.4 %collective-permute-start.19 = (bf16[512,128]{1,0:T(8,128)(2,1)S(1)}, bf16[512,128]{1,0:T(8,128)(2,1)S(1)}, u32[]{:S(2)}, u32[]{:S(2)}) collective-permute-start(bf16[512,128]{1,0:T(8,128)(2,1)S(1)} %add_convert_fusion.1), channel_id=1, source_target_pairs={{0,16},{1,17},{8,24},{9,25},{16,0},{17,1},{24,8},{25,9},{2,18},{3,... | collective-permute-start | bytes 393224 | tf_op jit(solution)/shard_map/ppermute | solution.py:115
  65.0 0.7 maximum_convert_fusion.2
  65.7 2.3 %fusion.2 = f32[1024,1024]{1,0:T(8,128)S(1)} fusion(bf16[1024,1024]{1,0:T(8,128)(2,1)S(1)} %maximum_convert_fusion.2, bf16[1024,4096]{1,0:T(8,128)(2,1)S(1)} %place_t.1), kind=kOutput, calls=%fused_computation.7 | convolution fusion | flops 2147483648 | bytes 8388608 | tf_op jit(solution)/shard_map/dot_general | solution.py:123
  68.0 0.7 maximum_convert_fusion.1
  68.7 2.3 %fusion = f32[1024,1024]{1,0:T(8,128)S(1)} fusion(bf16[1024,1024]{1,0:T(8,128)(2,1)S(1)} %maximum_convert_fusion.1, bf16[1024,4096]{1,0:T(8,128)(2,1)S(1)} %place_t.1), kind=kOutput, calls=%fused_computation.5 | convolution fusion | flops 2147483648 | bytes 8388608 | tf_op jit(solution)/shard_map/dot_general | solution.py:123
  71.1 0.7 maximum_convert_fusion
  71.8 0.8 add_add_fusion.1
  72.6 3.7 %collective-permute-start.21 = (bf16[128,1024]{1,0:T(8,128)(2,1)S(1)}, bf16[128,1024]{1,0:T(8,128)(2,1)S(1)}, u32[]{:S(2)}, u32[]{:S(2)}) collective-permute-start(bf16[128,1024]{1,0:T(8,128)(2,1)S(1)} %slice.216), channel_id=1, source_target_pairs={{0,32},{32,0},{1,33},{33,1},{2,34},{34,2},{3,35},{35,3},{4,36},{36... | collective-permute-start | bytes 786440 | tf_op jit(solution)/shard_map/ppermute | solution.py:22
  76.3 1.0 %add_convert_fusion = bf16[384,1024]{1,0:T(8,128)(2,1)S(1)} fusion(f32[1024,1024]{1,0:T(8,128)S(1)} %fusion, f32[1024,1024]{1,0:T(8,128)S(1)} %fusion.2, f32[1024,1024]{1,0:T(8,128)S(1)} %fusion.4, bf16[1024,1024]{1,0:T(8,128)(2,1)S(1)} %maximum_convert_fusion, bf16[1024,4096]{1,0:T(8,128)(2,1)S(1)} %place_t.1), kind=kOutput, calls=%fused_computation.11 | convolution fusion | flops 806879232 | bytes 8388608 | tf_op jit(solution)/shard_map/dot_general | solution.py:123
  77.5 2.3 %collective-permute-start.23 = (bf16[128,1024]{1,0:T(8,128)(2,1)S(1)}, bf16[128,1024]{1,0:T(8,128)(2,1)S(1)}, u32[]{:S(2)}, u32[]{:S(2)}) collective-permute-start(bf16[128,1024]{1,0:T(8,128)(2,1)S(1)} %fusion.21), channel_id=1, source_target_pairs={{0,128},{64,192},{128,0},{192,64},{1,129},{65,193},{129,1},{193,65... | collective-permute-start | bytes 786440 | tf_op jit(solution)/shard_map/ppermute | solution.py:22
  79.8 0.7 collective-permute-start.22
  80.6 0.4 collective-permute-start.24
  81.0 1.0 %add_add_fusion = f32[384,1024]{1,0:T(8,128)S(1)} fusion(f32[1024,1024]{1,0:T(8,128)S(1)} %fusion, f32[1024,1024]{1,0:T(8,128)S(1)} %fusion.2, f32[1024,1024]{1,0:T(8,128)S(1)} %fusion.4, bf16[1024,1024]{1,0:T(8,128)(2,1)S(1)} %maximum_convert_fusion, bf16[1024,4096]{1,0:T(8,128)(2,1)S(1)} %place_t.1), kind=kOutput, calls=%fused_computation.12 | convolution fusion | flops 806486016 | bytes 9175040 | tf_op jit(solution)/shard_map/dot_general | solution.py:123
  82.6 1.0 %collective-permute-start.25 = (bf16[128,1024]{1,0:T(8,128)(2,1)S(1)}, bf16[128,1024]{1,0:T(8,128)(2,1)S(1)}, u32[]{:S(2)}, u32[]{:S(2)}) collective-permute-start(bf16[128,1024]{1,0:T(8,128)(2,1)S(1)} %get-tuple-element.55), channel_id=1, source_target_pairs={{0,64},{64,128},{128,192},{192,0},{1,65},{65,129},{129,193},{193,1... | collective-permute-start | bytes 786440 | tf_op jit(solution)/shard_map/ppermute | solution.py:22
  83.6 1.8 %collective-permute-start.27 = (bf16[128,1024]{1,0:T(8,128)(2,1)S(1)}, bf16[128,1024]{1,0:T(8,128)(2,1)S(1)}, u32[]{:S(2)}, u32[]{:S(2)}) collective-permute-start(bf16[128,1024]{1,0:T(8,128)(2,1)S(1)} %get-tuple-element.56), channel_id=1, source_target_pairs={{0,192},{64,0},{128,64},{192,128},{1,193},{65,1},{129,65},{193,129... | collective-permute-start | bytes 786440 | tf_op jit(solution)/shard_map/ppermute | solution.py:22
  85.4 1.2 %collective-permute-done.23 = bf16[128,1024]{1,0:T(8,128)(2,1)S(1)} collective-permute-done((bf16[128,1024]{1,0:T(8,128)(2,1)S(1)}, bf16[128,1024]{1,0:T(8,128)(2,1)S(1)}, u32[]{:S(2)}, u32[]{:S(2)}) %collective-permute-start.23) | collective-permute-done | bytes 262176 | tf_op jit(solution)/shard_map/ppermute | solution.py:22
  86.6 6.0 %collective-permute-done.25 = bf16[128,1024]{1,0:T(8,128)(2,1)S(1)} collective-permute-done((bf16[128,1024]{1,0:T(8,128)(2,1)S(1)}, bf16[128,1024]{1,0:T(8,128)(2,1)S(1)}, u32[]{:S(2)}, u32[]{:S(2)}) %collective-permute-start.25) | collective-permute-done | bytes 262176 | tf_op jit(solution)/shard_map/ppermute | solution.py:22
  92.6 1.2 %fusion.6 = bf16[128,1024]{1,0:T(8,128)(2,1)} fusion(bf16[1024,1024]{1,0:T(8,128)(2,1)S(1)} %copy-done, f32[384,1024]{1,0:T(8,128)S(1)} %add_add_fusion, bf16[128,1024]{1,0:T(8,128)(2,1)S(1)} %collective-permute-done.27, bf16[128,1024]{1,0:T(8,128)(2,1)S(1)} %collective-permute-done.25, bf16[128,1024]{1,0:T(8,128)(2,1)S(1)} %collective-permute-done.23, ...), kind=kOutput, calls=%fused_computation.14 | convolution fusion | flops 269877248 | bytes 3932160 | tf_op jit(solution)/shard_map/dot_general | solution.py:156
  (43 shorter events, 2.0 us)
Async XLA Ops:
  0.0 92.6 %copy-start = (bf16[1024,1024]{1,0:T(8,128)(2,1)S(1)}, bf16[1024,1024]{1,0:T(8,128)(2,1)}, u32[]{:S(2)}) copy-start(bf16[1024,1024]{1,0:T(8,128)(2,1)} %param.13) | copy-start | bytes 6291460
  0.0 4.7 %collective-permute-start = (bf16[128,128]{1,0:T(8,128)(2,1)}, bf16[128,128]{1,0:T(8,128)(2,1)S(1)}, u32[]{:S(2)}, u32[]{:S(2)}) collective-permute-start(bf16[128,128]{1,0:T(8,128)(2,1)} %param.7), channel_id=1, source_target_pairs={{0,32},{32,0},{1,33},{33,1},{2,34},{34,2},{3,35},{35,3},{4,36},{36... | collective-permute-start | bytes 98312 | tf_op jit(solution)/shard_map/ppermute | solution.py:22
  4.7 5.1 %collective-permute-start.1 = (bf16[256,128]{1,0:T(8,128)(2,1)S(1)}, bf16[256,128]{1,0:T(8,128)(2,1)S(1)}, u32[]{:S(2)}, u32[]{:S(2)}) collective-permute-start(bf16[256,128]{1,0:T(8,128)(2,1)S(1)} %constant_dynamic-update-slice_fusion), channel_id=1, source_target_pairs={{0,128},{64,192},{128,0},{192,64},{1,129},{65,193},{129,1},{193,65... | collective-permute-start | bytes 196616 | tf_op jit(solution)/shard_map/ppermute | solution.py:22
  6.7 6.1 %collective-permute-start.3 = (bf16[256,128]{1,0:T(8,128)(2,1)S(1)}, bf16[256,128]{1,0:T(8,128)(2,1)S(1)}, u32[]{:S(2)}, u32[]{:S(2)}) collective-permute-start(bf16[256,128]{1,0:T(8,128)(2,1)S(1)} %constant_dynamic-update-slice_fusion), channel_id=1, source_target_pairs={{0,64},{64,128},{128,192},{192,0},{1,65},{65,129},{129,193},{193,1... | collective-permute-start | bytes 196616 | tf_op jit(solution)/shard_map/ppermute | solution.py:22
  7.1 5.7 %collective-permute-start.2 = (bf16[256,128]{1,0:T(8,128)(2,1)S(1)}, bf16[256,128]{1,0:T(8,128)(2,1)S(1)}, u32[]{:S(2)}, u32[]{:S(2)}) collective-permute-start(bf16[256,128]{1,0:T(8,128)(2,1)S(1)} %constant_dynamic-update-slice_fusion), channel_id=1, source_target_pairs={{0,192},{64,0},{128,64},{192,128},{1,193},{65,1},{129,65},{193,129... | collective-permute-start | bytes 196616 | tf_op jit(solution)/shard_map/ppermute | solution.py:22
  15.5 8.5 %collective-permute-start.4 = (bf16[512,128]{1,0:T(8,128)(2,1)S(1)}, bf16[512,128]{1,0:T(8,128)(2,1)S(1)}, u32[]{:S(2)}, u32[]{:S(2)}) collective-permute-start(bf16[512,128]{1,0:T(8,128)(2,1)S(1)} %get-tuple-element.57), channel_id=1, source_target_pairs={{0,17},{1,16},{8,25},{9,24},{16,1},{17,0},{24,9},{25,8},{2,19},{3,... | collective-permute-start | bytes 393224 | tf_op jit(solution)/shard_map/ppermute | solution.py:105
  19.3 5.5 %collective-permute-start.10 = (bf16[512,128]{1,0:T(8,128)(2,1)S(1)}, bf16[512,128]{1,0:T(8,128)(2,1)S(1)}, u32[]{:S(2)}, u32[]{:S(2)}) collective-permute-start(bf16[512,128]{1,0:T(8,128)(2,1)S(1)} %get-tuple-element.58), channel_id=1, source_target_pairs={{0,1},{1,0},{8,9},{9,8},{16,17},{17,16},{24,25},{25,24},{2,3},{3,2... | collective-permute-start | bytes 393224 | tf_op jit(solution)/shard_map/ppermute | solution.py:105
  19.3 7.2 %collective-permute-start.9 = (bf16[512,128]{1,0:T(8,128)(2,1)S(1)}, bf16[512,128]{1,0:T(8,128)(2,1)S(1)}, u32[]{:S(2)}, u32[]{:S(2)}) collective-permute-start(bf16[512,128]{1,0:T(8,128)(2,1)S(1)} %get-tuple-element.59), channel_id=1, source_target_pairs={{0,24},{1,25},{8,0},{9,1},{16,8},{17,9},{24,16},{25,17},{2,26},{3,... | collective-permute-start | bytes 393224 | tf_op jit(solution)/shard_map/ppermute | solution.py:105
  20.2 6.3 %collective-permute-start.8 = (bf16[512,128]{1,0:T(8,128)(2,1)S(1)}, bf16[512,128]{1,0:T(8,128)(2,1)S(1)}, u32[]{:S(2)}, u32[]{:S(2)}) collective-permute-start(bf16[512,128]{1,0:T(8,128)(2,1)S(1)} %get-tuple-element.60), channel_id=1, source_target_pairs={{0,8},{1,9},{8,16},{9,17},{16,24},{17,25},{24,0},{25,1},{2,10},{3,... | collective-permute-start | bytes 393224 | tf_op jit(solution)/shard_map/ppermute | solution.py:105
  20.8 6.9 %collective-permute-start.7 = (bf16[512,128]{1,0:T(8,128)(2,1)S(1)}, bf16[512,128]{1,0:T(8,128)(2,1)S(1)}, u32[]{:S(2)}, u32[]{:S(2)}) collective-permute-start(bf16[512,128]{1,0:T(8,128)(2,1)S(1)} %get-tuple-element.61), channel_id=1, source_target_pairs={{0,25},{1,24},{8,1},{9,0},{16,9},{17,8},{24,17},{25,16},{2,27},{3,... | collective-permute-start | bytes 393224 | tf_op jit(solution)/shard_map/ppermute | solution.py:105
  24.0 7.0 %collective-permute-start.6 = (bf16[512,128]{1,0:T(8,128)(2,1)S(1)}, bf16[512,128]{1,0:T(8,128)(2,1)S(1)}, u32[]{:S(2)}, u32[]{:S(2)}) collective-permute-start(bf16[512,128]{1,0:T(8,128)(2,1)S(1)} %get-tuple-element.62), channel_id=1, source_target_pairs={{0,9},{1,8},{8,17},{9,16},{16,25},{17,24},{24,1},{25,0},{2,11},{3,... | collective-permute-start | bytes 393224 | tf_op jit(solution)/shard_map/ppermute | solution.py:105
  24.8 7.9 %collective-permute-start.5 = (bf16[512,128]{1,0:T(8,128)(2,1)S(1)}, bf16[512,128]{1,0:T(8,128)(2,1)S(1)}, u32[]{:S(2)}, u32[]{:S(2)}) collective-permute-start(bf16[512,128]{1,0:T(8,128)(2,1)S(1)} %get-tuple-element.63), channel_id=1, source_target_pairs={{0,16},{1,17},{8,24},{9,25},{16,0},{17,1},{24,8},{25,9},{2,18},{3,... | collective-permute-start | bytes 393224 | tf_op jit(solution)/shard_map/ppermute | solution.py:105
  32.8 21.7 %copy-start.1 = (bf16[128,1024]{1,0:T(8,128)(2,1)S(1)}, bf16[128,1024]{1,0:T(8,128)(2,1)}, u32[]{:S(2)}) copy-start(bf16[128,1024]{1,0:T(8,128)(2,1)} %param.12) | copy-start | bytes 786436
  32.9 8.1 %collective-permute-start.11 = (bf16[512,128]{1,0:T(8,128)(2,1)S(1)}, bf16[512,128]{1,0:T(8,128)(2,1)S(1)}, u32[]{:S(2)}, u32[]{:S(2)}) collective-permute-start(bf16[512,128]{1,0:T(8,128)(2,1)S(1)} %add_convert_fusion.2), channel_id=1, source_target_pairs={{0,4},{2,6},{4,0},{6,2},{1,5},{3,7},{5,1},{7,3},{8,12},{10,14},{12... | collective-permute-start | bytes 393224 | tf_op jit(solution)/shard_map/ppermute | solution.py:22
  38.2 12.3 %collective-permute-start.13 = (bf16[512,128]{1,0:T(8,128)(2,1)S(1)}, bf16[512,128]{1,0:T(8,128)(2,1)S(1)}, u32[]{:S(2)}, u32[]{:S(2)}) collective-permute-start(bf16[512,128]{1,0:T(8,128)(2,1)S(1)} %add_convert_fusion.2), channel_id=1, source_target_pairs={{0,6},{2,0},{4,2},{6,4},{1,7},{3,1},{5,3},{7,5},{8,14},{10,8},{12,... | collective-permute-start | bytes 393224 | tf_op jit(solution)/shard_map/ppermute | solution.py:22
  38.2 12.3 %collective-permute-start.12 = (bf16[512,128]{1,0:T(8,128)(2,1)S(1)}, bf16[512,128]{1,0:T(8,128)(2,1)S(1)}, u32[]{:S(2)}, u32[]{:S(2)}) collective-permute-start(bf16[512,128]{1,0:T(8,128)(2,1)S(1)} %add_convert_fusion.2), channel_id=1, source_target_pairs={{0,2},{2,4},{4,6},{6,0},{1,3},{3,5},{5,7},{7,1},{8,10},{10,12},{12... | collective-permute-start | bytes 393224 | tf_op jit(solution)/shard_map/ppermute | solution.py:22
  50.6 3.9 %collective-permute-start.14 = (bf16[512,128]{1,0:T(8,128)(2,1)S(1)}, bf16[512,128]{1,0:T(8,128)(2,1)S(1)}, u32[]{:S(2)}, u32[]{:S(2)}) collective-permute-start(bf16[512,128]{1,0:T(8,128)(2,1)S(1)} %add_convert_fusion.1), channel_id=1, source_target_pairs={{0,1},{1,0},{8,9},{9,8},{16,17},{17,16},{24,25},{25,24},{2,3},{3,2... | collective-permute-start | bytes 393224 | tf_op jit(solution)/shard_map/ppermute | solution.py:115
  51.6 9.7 %collective-permute-start.16 = (bf16[512,128]{1,0:T(8,128)(2,1)S(1)}, bf16[512,128]{1,0:T(8,128)(2,1)S(1)}, u32[]{:S(2)}, u32[]{:S(2)}) collective-permute-start(bf16[512,128]{1,0:T(8,128)(2,1)S(1)} %add_convert_fusion.1), channel_id=1, source_target_pairs={{0,8},{1,9},{8,16},{9,17},{16,24},{17,25},{24,0},{25,1},{2,10},{3,... | collective-permute-start | bytes 393224 | tf_op jit(solution)/shard_map/ppermute | solution.py:115
  53.1 8.3 %collective-permute-start.15 = (bf16[512,128]{1,0:T(8,128)(2,1)S(1)}, bf16[512,128]{1,0:T(8,128)(2,1)S(1)}, u32[]{:S(2)}, u32[]{:S(2)}) collective-permute-start(bf16[512,128]{1,0:T(8,128)(2,1)S(1)} %add_convert_fusion.1), channel_id=1, source_target_pairs={{0,24},{1,25},{8,0},{9,1},{16,8},{17,9},{24,16},{25,17},{2,26},{3,... | collective-permute-start | bytes 393224 | tf_op jit(solution)/shard_map/ppermute | solution.py:115
  55.2 12.7 %collective-permute-start.18 = (bf16[512,128]{1,0:T(8,128)(2,1)S(1)}, bf16[512,128]{1,0:T(8,128)(2,1)S(1)}, u32[]{:S(2)}, u32[]{:S(2)}) collective-permute-start(bf16[512,128]{1,0:T(8,128)(2,1)S(1)} %add_convert_fusion.1), channel_id=1, source_target_pairs={{0,9},{1,8},{8,17},{9,16},{16,25},{17,24},{24,1},{25,0},{2,11},{3,... | collective-permute-start | bytes 393224 | tf_op jit(solution)/shard_map/ppermute | solution.py:115
  58.1 9.9 %collective-permute-start.17 = (bf16[512,128]{1,0:T(8,128)(2,1)S(1)}, bf16[512,128]{1,0:T(8,128)(2,1)S(1)}, u32[]{:S(2)}, u32[]{:S(2)}) collective-permute-start(bf16[512,128]{1,0:T(8,128)(2,1)S(1)} %add_convert_fusion.1), channel_id=1, source_target_pairs={{0,25},{1,24},{8,1},{9,0},{16,9},{17,8},{24,17},{25,16},{2,27},{3,... | collective-permute-start | bytes 393224 | tf_op jit(solution)/shard_map/ppermute | solution.py:115
  61.4 9.7 %collective-permute-start.20 = (bf16[512,128]{1,0:T(8,128)(2,1)S(1)}, bf16[512,128]{1,0:T(8,128)(2,1)S(1)}, u32[]{:S(2)}, u32[]{:S(2)}) collective-permute-start(bf16[512,128]{1,0:T(8,128)(2,1)S(1)} %add_convert_fusion.1), channel_id=1, source_target_pairs={{0,17},{1,16},{8,25},{9,24},{16,1},{17,0},{24,9},{25,8},{2,19},{3,... | collective-permute-start | bytes 393224 | tf_op jit(solution)/shard_map/ppermute | solution.py:115
  62.5 8.5 %collective-permute-start.19 = (bf16[512,128]{1,0:T(8,128)(2,1)S(1)}, bf16[512,128]{1,0:T(8,128)(2,1)S(1)}, u32[]{:S(2)}, u32[]{:S(2)}) collective-permute-start(bf16[512,128]{1,0:T(8,128)(2,1)S(1)} %add_convert_fusion.1), channel_id=1, source_target_pairs={{0,16},{1,17},{8,24},{9,25},{16,0},{17,1},{24,8},{25,9},{2,18},{3,... | collective-permute-start | bytes 393224 | tf_op jit(solution)/shard_map/ppermute | solution.py:115
  72.6 4.8 %collective-permute-start.21 = (bf16[128,1024]{1,0:T(8,128)(2,1)S(1)}, bf16[128,1024]{1,0:T(8,128)(2,1)S(1)}, u32[]{:S(2)}, u32[]{:S(2)}) collective-permute-start(bf16[128,1024]{1,0:T(8,128)(2,1)S(1)} %slice.216), channel_id=1, source_target_pairs={{0,32},{32,0},{1,33},{33,1},{2,34},{34,2},{3,35},{35,3},{4,36},{36... | collective-permute-start | bytes 786440 | tf_op jit(solution)/shard_map/ppermute | solution.py:22
  77.5 9.1 %collective-permute-start.23 = (bf16[128,1024]{1,0:T(8,128)(2,1)S(1)}, bf16[128,1024]{1,0:T(8,128)(2,1)S(1)}, u32[]{:S(2)}, u32[]{:S(2)}) collective-permute-start(bf16[128,1024]{1,0:T(8,128)(2,1)S(1)} %fusion.21), channel_id=1, source_target_pairs={{0,128},{64,192},{128,0},{192,64},{1,129},{65,193},{129,1},{193,65... | collective-permute-start | bytes 786440 | tf_op jit(solution)/shard_map/ppermute | solution.py:22
  79.8 6.8 %collective-permute-start.22 = (bf16[128,1024]{1,0:T(8,128)(2,1)S(1)}, bf16[128,1024]{1,0:T(8,128)(2,1)S(1)}, u32[]{:S(2)}, u32[]{:S(2)}) collective-permute-start(bf16[128,1024]{1,0:T(8,128)(2,1)S(1)} %get-tuple-element.64), channel_id=1, source_target_pairs={{0,32},{32,0},{1,33},{33,1},{2,34},{34,2},{3,35},{35,3},{4,36},{36... | collective-permute-start | bytes 786440 | tf_op jit(solution)/shard_map/ppermute | solution.py:22
  80.5 1.5 %collective-permute-start.26 = (bf16[128,1024]{1,0:T(8,128)(2,1)S(1)}, bf16[128,1024]{1,0:T(8,128)(2,1)S(1)}, u32[]{:S(2)}, u32[]{:S(2)}) collective-permute-start(bf16[128,1024]{1,0:T(8,128)(2,1)S(1)} %get-tuple-element.65), channel_id=1, source_target_pairs={{0,32},{32,0},{1,33},{33,1},{2,34},{34,2},{3,35},{35,3},{4,36},{36... | collective-permute-start | bytes 786440 | tf_op jit(solution)/shard_map/ppermute | solution.py:22
  80.6 1.8 %collective-permute-start.24 = (bf16[128,1024]{1,0:T(8,128)(2,1)S(1)}, bf16[128,1024]{1,0:T(8,128)(2,1)S(1)}, u32[]{:S(2)}, u32[]{:S(2)}) collective-permute-start(bf16[128,1024]{1,0:T(8,128)(2,1)S(1)} %get-tuple-element.66), channel_id=1, source_target_pairs={{0,32},{32,0},{1,33},{33,1},{2,34},{34,2},{3,35},{35,3},{4,36},{36... | collective-permute-start | bytes 786440 | tf_op jit(solution)/shard_map/ppermute | solution.py:22
  82.6 10.0 %collective-permute-start.25 = (bf16[128,1024]{1,0:T(8,128)(2,1)S(1)}, bf16[128,1024]{1,0:T(8,128)(2,1)S(1)}, u32[]{:S(2)}, u32[]{:S(2)}) collective-permute-start(bf16[128,1024]{1,0:T(8,128)(2,1)S(1)} %get-tuple-element.55), channel_id=1, source_target_pairs={{0,64},{64,128},{128,192},{192,0},{1,65},{65,129},{129,193},{193,1... | collective-permute-start | bytes 786440 | tf_op jit(solution)/shard_map/ppermute | solution.py:22
  83.6 9.0 %collective-permute-start.27 = (bf16[128,1024]{1,0:T(8,128)(2,1)S(1)}, bf16[128,1024]{1,0:T(8,128)(2,1)S(1)}, u32[]{:S(2)}, u32[]{:S(2)}) collective-permute-start(bf16[128,1024]{1,0:T(8,128)(2,1)S(1)} %get-tuple-element.56), channel_id=1, source_target_pairs={{0,192},{64,0},{128,64},{192,128},{1,193},{65,1},{129,65},{193,129... | collective-permute-start | bytes 786440 | tf_op jit(solution)/shard_map/ppermute | solution.py:22
